TPU v7x, 32 devices: a whole 2x2x4 slice. The times are simulated.
32 devices in a mesh: clip: 2 (over y), fp: 4 (over z), tp: 4 (over x, core).
Axes of the slice: x: 2, y: 2, z: 4, core: 2. Of those that a mesh axis runs over, the one named last changes fastest.
Arguments:
- inputs: bfloat16 [2, 8, 16, 192, 768], P(None, 'clip', 'fp', 'tp'), may hold values from -6 to 6
- cotangent: bfloat16 [2, 8, 16, 192, 768], P(None, 'clip', 'fp', 'tp'), may hold values from -6 to 6
- qkv_weight: bfloat16 [2, 3, 768, 768], P(None, None, ('clip', 'fp'), 'tp'), may hold values from -0.21875 to 0.21875
- out_spatial: bfloat16 [768, 768], P('tp', ('clip', 'fp')), may hold values from -1.5 to 1.5
- out_temporal: bfloat16 [768, 768], P('tp', ('clip', 'fp')), may hold values from -0.4375 to 0.4375
- mlp_in: bfloat16 [768, 3072], P(('clip', 'fp'), 'tp'), may hold values from -0.21875 to 0.21875
- mlp_out: bfloat16 [3072, 768], P('tp', ('clip', 'fp')), may hold values from -0.15625 to 0.15625
- ln_gain: bfloat16 [3, 768], P(None, ('clip', 'fp')), may hold values from 0.5 to 1.5
- ln_bias: bfloat16 [3, 768], P(None, ('clip', 'fp')), may hold values from -2 to 2
Outputs:
- activations: bfloat16 [2, 8, 16, 192, 768], P(None, 'clip', 'fp', 'tp')
- input_grad: float32 [2, 8, 16, 192, 768], P(None, 'clip', 'fp', 'tp')
- qkv_grad: float32 [2, 3, 768, 768], P(None, None, ('clip', 'fp'), 'tp')
- out_spatial_grad: float32 [768, 768], P('tp', ('clip', 'fp'))
- out_temporal_grad: float32 [768, 768], P('tp', ('clip', 'fp'))
- mlp_in_grad: float32 [768, 3072], P(('clip', 'fp'), 'tp')
- mlp_out_grad: float32 [3072, 768], P('tp', ('clip', 'fp'))
- ln_gain_grad: float32 [3, 768], P(None, ('clip', 'fp'))
- ln_bias_grad: float32 [3, 768], P(None, ('clip', 'fp'))
All inputs are finite; a program needn't handle non-finite values.
Results may differ from a plain program's by a relative error of at most 0.014.
Values may be sent and summed in bfloat16 or wider, within the bound.
A program may use at most 320 MiB of HBM per device.

v0:
```python
from functools import partial

import jax
import jax.numpy as jnp
from jax import lax
from jax.experimental import pallas as pl
from jax.experimental.pallas import tpu as pltpu
from jax.sharding import PartitionSpec as P

HD = 64
GROUP = 4
WIDE = GROUP * HD
EPS = 1e-06
BF = jnp.bfloat16
F32 = jnp.float32
MIB = 1024 * 1024
MESH = pl.DeviceIdType.MESH

NN = (((1,), (0,)), ((), ()))
NT = (((1,), (1,)), ((), ()))
TN = (((0,), (0,)), ((), ()))


def dot(a, b, dims):
    return lax.dot_general(a, b, dims, preferred_element_type=F32)


def normalise(values):
    centre = values - jnp.mean(values, axis=-1, keepdims=True)
    spread = jnp.mean(centre * centre, axis=-1, keepdims=True)
    rate = lax.rsqrt(spread + EPS)
    return centre * rate, rate


def norm_back(upstream, gain, unit, rate):
    weighted = upstream * gain
    inner = jnp.mean(weighted * unit, axis=-1, keepdims=True)
    return rate * (weighted - jnp.mean(weighted, axis=-1, keepdims=True) - unit * inner)


def head_masks(scale):
    lanes = lax.broadcasted_iota(jnp.int32, (1, WIDE), 1) // HD
    return [jnp.where(lanes == h, scale, 0.0).astype(BF) for h in range(GROUP)]


def spread_heads(block, masks):
    return jnp.concatenate([block * mask for mask in masks], axis=0)


def gather_heads(stacked, rows):
    lanes = lax.broadcasted_iota(jnp.int32, (1, WIDE), 1) // HD
    total = stacked[:rows]
    for h in range(1, GROUP):
        total = jnp.where(lanes == h, stacked[h * rows : (h + 1) * rows], total)
    return total


def attend(queries, keys, values, bias):
    rows = queries.shape[0]
    scores = dot(keys, spread_heads(queries, head_masks(HD**-0.5)), NT)
    if bias is not None:
        scores = scores + bias
    top = jnp.max(scores, axis=0, keepdims=True)
    exponent = jnp.exp(scores - top)
    totals = jnp.sum(exponent, axis=0, keepdims=True)
    weights = (exponent * (1.0 / totals)).astype(BF)
    mixed = gather_heads(dot(weights, values, TN), rows).astype(BF)
    return mixed, top + jnp.log(totals)


def attend_back(queries, keys, values, upstream, logsum, bias):
    rows = queries.shape[0]
    spread_q = spread_heads(queries, head_masks(HD**-0.5))
    spread_g = spread_heads(upstream, head_masks(1.0))
    scores = dot(keys, spread_q, NT)
    if bias is not None:
        scores = scores + bias
    probs = jnp.exp(scores - logsum)
    grad_probs = dot(values, spread_g, NT)
    inner = jnp.sum(probs * grad_probs, axis=0, keepdims=True)
    grad_scores = (probs * (grad_probs - inner)).astype(BF)
    grad_values = dot(probs.astype(BF), spread_g, NN)
    grad_keys = dot(grad_scores, spread_q, NN)
    grad_queries = gather_heads(dot(grad_scores, keys, TN), rows) * HD**-0.5
    return grad_queries.astype(BF), grad_keys.astype(BF), grad_values.astype(BF)


def gelu_parts(pre):
    size = jnp.abs(pre) * (0.5**0.5)
    t = 1.0 / (1.0 + 0.3275911 * size)
    bell = jnp.exp(-size * size)
    poly = t * (
        0.254829592
        + t * (-0.284496736 + t * (1.421413741 + t * (-1.453152027 + t * 1.061405429)))
    )
    tail = 0.5 * poly * bell
    return jnp.where(pre >= 0, 1.0 - tail, tail), bell * 0.3989422804014327


def space_forward_kernel(n_in, n_out, at_ref, *refs):
    pieces = refs[:n_in]
    qkv_w, out_w, norm = refs[n_in : n_in + 3]
    outs = refs[n_in + 3 : n_in + 3 + n_out]
    qkv_out, mixed_out, logsum_out, held = refs[n_in + 3 + n_out :]
    width = out_w.shape[1]
    x = jnp.concatenate([piece[0] for piece in pieces], axis=0).astype(F32)
    unit, _ = normalise(x)
    normed = (unit * norm[0:1] + norm[1:2]).astype(BF)
    qkv_out[0] = dot(normed, qkv_w[...], NN).astype(BF)
    for g in range(width // WIDE):
        at = g * WIDE
        mixed, logsum = attend(
            qkv_out[0, :, at : at + WIDE],
            qkv_out[0, :, width + at : width + at + WIDE],
            qkv_out[0, :, 2 * width + at : 2 * width + at + WIDE],
            None,
        )
        mixed_out[0, :, at : at + WIDE] = mixed
        logsum_out[0, g : g + 1] = logsum
    held[...] = x + dot(mixed_out[0], out_w[...], NT)
    rows = outs[0].shape[1]
    for r, out in enumerate(outs):
        start = pl.multiple_of((at_ref[0] ^ r) * rows, 8)
        out[0] = held[pl.ds(start, rows), :].astype(BF)


def space_forward(pieces, qkv_w, out_w, norm, at, n_out):
    frames, rows, width = pieces[0].shape
    places = rows * len(pieces)
    groups = width // WIDE
    whole = pl.BlockSpec(memory_space=pltpu.VMEM)
    frame = lambda *dims: pl.BlockSpec((1,) + dims, lambda f, at: (f,) + (0,) * len(dims))
    return pl.pallas_call(
        partial(space_forward_kernel, len(pieces), n_out),
        grid_spec=pltpu.PrefetchScalarGridSpec(
            num_scalar_prefetch=1,
            grid=(frames,),
            in_specs=[frame(rows, width)] * len(pieces) + [whole] * 3,
            out_specs=[frame(places // n_out, width)] * n_out
            + [frame(places, 3 * width), frame(places, width), frame(groups, GROUP * places)],
            scratch_shapes=[pltpu.VMEM((places, width), F32)],
        ),
        out_shape=[jax.ShapeDtypeStruct((frames, places // n_out, width), BF)] * n_out
        + [
            jax.ShapeDtypeStruct((frames, places, 3 * width), BF),
            jax.ShapeDtypeStruct((frames, places, width), BF),
            jax.ShapeDtypeStruct((frames, groups, GROUP * places), F32),
        ],
        compiler_params=pltpu.CompilerParams(vmem_limit_bytes=48 * MIB),
        cost_estimate=pl.CostEstimate(
            flops=2 * frames * places * width * 5 * width,
            bytes_accessed=frames * places * width * 16,
            transcendentals=0,
        ),
    )(at, *pieces, qkv_w, out_w, norm)


def store_columns(out, kinds, n_parts):
    width = kinds[0].shape[1]
    span = width // n_parts
    for t in range(n_parts):
        for i, kind in enumerate(kinds):
            start = (t * len(kinds) + i) * span
            out[:, start : start + span] = kind[:, t * span : (t + 1) * span]


def space_backward_kernel(n_in, n_grad, n_out, at_ref, *refs):
    pieces = refs[:n_in]
    grads = refs[n_in : n_in + n_grad]
    qkv_in, mixed_in, logsum_in, qkv_w, out_w, norm = refs[n_in + n_grad : n_in + n_grad + 6]
    rest = refs[n_in + n_grad + 6 :]
    outs = rest[:n_out]
    normed_out, grad_out, columns, norm_out, held, dqkv = rest[n_out:]
    width = out_w.shape[1]
    rows = grads[0].shape[1]
    for r, grad in enumerate(grads):
        start = pl.multiple_of((at_ref[0] ^ r) * rows, 8)
        held[pl.ds(start, rows), :] = grad[0].astype(F32)
    x = jnp.concatenate([piece[0] for piece in pieces], axis=0).astype(F32)
    unit, rate = normalise(x)
    normed_out[0] = (unit * norm[0:1] + norm[1:2]).astype(BF)
    low = held[...].astype(BF)
    grad_out[0] = low
    grad_mixed = dot(low, out_w[...], NN).astype(BF)
    for g in range(width // WIDE):
        at = g * WIDE
        parts = attend_back(
            qkv_in[0, :, at : at + WIDE],
            qkv_in[0, :, width + at : width + at + WIDE],
            qkv_in[0, :, 2 * width + at : 2 * width + at + WIDE],
            grad_mixed[:, at : at + WIDE],
            logsum_in[0, g : g + 1],
            None,
        )
        for i, part in enumerate(parts):
            dqkv[:, i * width + at : i * width + at + WIDE] = part
    store_columns(
        columns.at[0],
        [dqkv[:, i * width : (i + 1) * width] for i in range(3)] + [mixed_in[0]],
        n_out,
    )
    grad_normed = dot(dqkv[...], qkv_w[...], NT)

    @pl.when(pl.program_id(0) == 0)
    def _():
        norm_out[...] = jnp.zeros_like(norm_out)

    norm_out[0:1] += jnp.sum(grad_normed * unit, axis=0, keepdims=True)
    norm_out[1:2] += jnp.sum(grad_normed, axis=0, keepdims=True)
    total = held[...] + norm_back(grad_normed, norm[0:1], unit, rate)
    rows = outs[0].shape[1]
    for s, out in enumerate(outs):
        out[0] = total[s * rows : (s + 1) * rows].astype(BF)


def space_backward(pieces, grads, qkv, mixed, logsum, qkv_w, out_w, norm, at, first, n_out):
    frames, width = grads[0].shape[0], grads[0].shape[2]
    places = grads[0].shape[1] * len(grads)
    rows = places // n_out
    groups = width // WIDE
    n_grad = len(grads)
    whole = pl.BlockSpec(memory_space=pltpu.VMEM)
    frame = lambda *dims: pl.BlockSpec((1,) + dims, lambda f, at: (f,) + (0,) * len(dims))
    later = lambda *dims: pl.BlockSpec((1,) + dims, lambda f, at: (f + first,) + (0,) * len(dims))
    return pl.pallas_call(
        partial(space_backward_kernel, len(pieces), n_grad, n_out),
        grid_spec=pltpu.PrefetchScalarGridSpec(
            num_scalar_prefetch=1,
            grid=(frames,),
            in_specs=[later(places // len(pieces), width)] * len(pieces)
            + [frame(places // n_grad, width)] * n_grad
            + [later(places, 3 * width), later(places, width), later(groups, GROUP * places)]
            + [whole] * 3,
            out_specs=[frame(rows, width)] * n_out
            + [frame(places, width), frame(places, width), frame(places, 4 * width)]
            + [pl.BlockSpec((2, width), lambda f, at: (0, 0))],
            scratch_shapes=[
                pltpu.VMEM((places, width), F32),
                pltpu.VMEM((places, 3 * width), BF),
            ],
        ),
        out_shape=[jax.ShapeDtypeStruct((frames, rows, width), BF)] * n_out
        + [
            jax.ShapeDtypeStruct((frames, places, width), BF),
            jax.ShapeDtypeStruct((frames, places, width), BF),
            jax.ShapeDtypeStruct((frames, places, 4 * width), BF),
            jax.ShapeDtypeStruct((2, width), F32),
        ],
        compiler_params=pltpu.CompilerParams(vmem_limit_bytes=48 * MIB),
        cost_estimate=pl.CostEstimate(
            flops=2 * frames * places * width * 7 * width,
            bytes_accessed=frames * places * width * 24,
            transcendentals=0,
        ),
    )(at, *pieces, *grads, qkv, mixed, logsum, qkv_w, out_w, norm)


def time_kernel(joint, n_in, n_parts, sub, *refs):
    n_arrays = 1 if joint else n_in
    n_cots = 2 if joint else n_in
    n_moved = 2 if joint else n_in
    pieces = refs[:n_arrays]
    cots = refs[n_arrays : n_arrays + n_cots]
    qkv_w, out_w, in_w, unit_w, norm = refs[n_arrays + n_cots : n_arrays + n_cots + 5]
    rest = refs[n_arrays + n_cots + 5 :]
    results = rest[:n_arrays]
    grads = rest[n_arrays : n_arrays + n_moved]
    rest = rest[n_arrays + n_moved :]
    (
        normed_time,
        columns,
        grad_time,
        normed_mlp,
        grad_pre,
        hidden,
        grad_result,
        norm_out,
        qkv,
        dqkv,
        mixed,
        probs_logsum,
    ) = rest[:12]
    if joint:
        step, steps = pl.program_id(0), pl.num_programs(0)
        outgoing, cot_in, send, recv, c_send, c_recv, cot_sem = rest[12:]
        late = grads[1]
        my_z = lax.axis_index("fp")
        to_z = [{"fp": my_z ^ r} for r in range(n_in)]
        block = results[0].shape[-2]
        chunk = late.shape[2]
        each = chunk // block
        slot = lax.rem(step, 2)

        def late_copy(r):
            src = cots[1].at[:, pl.ds(pl.multiple_of((my_z ^ r) * chunk, 16), chunk)]
            if r == 0:
                return pltpu.make_async_copy(src, late.at[0], c_send.at[0])
            return pltpu.make_async_remote_copy(
                src_ref=src, dst_ref=late.at[r], send_sem=c_send.at[r], recv_sem=c_recv.at[r],
                device_id=to_z[r], device_id_type=MESH,
            )

        def cot_fetch(array, at, slot):
            rows = pl.ds(pl.multiple_of(at * block, 8), block)
            return pltpu.make_async_copy(
                array.at[:, :, rows], cot_in.at[slot], cot_sem.at[slot]
            )

        @pl.when(step == 0)
        def _():
            barrier = pltpu.get_barrier_semaphore()
            for peer in to_z[1:]:
                pl.semaphore_signal(barrier, inc=1, device_id=peer, device_id_type=MESH)
            pl.semaphore_wait(barrier, n_in - 1)
            for r in range(n_in):
                late_copy(r).start()
            cot_fetch(cots[0], 0, 0).start()

        @pl.when(jnp.logical_and(step + 1 < each, step + 1 < steps))
        def _():
            cot_fetch(cots[0], step + 1, 1 - slot).start()

    width = out_w.shape[1]
    frames, places = results[0].shape[-3:-1]
    all_frames = frames * n_in
    rows = all_frames * sub
    parts = places // sub

    def tokens(blocks):
        blocks = [b[...].reshape(-1, places, width) for b in blocks]
        joined = jnp.concatenate(blocks, axis=0).astype(F32)
        return jnp.concatenate(
            [joined[:, j * sub : (j + 1) * sub, :].reshape(rows, width) for j in range(parts)],
            axis=0,
        )

    def scatter(values, outs):
        grid = jnp.concatenate(
            [
                values[j * rows : (j + 1) * rows].reshape(all_frames, sub, width)
                for j in range(parts)
            ],
            axis=1,
        ).astype(BF)
        if len(outs) == 1:
            outs[0][...] = grid.reshape(outs[0].shape)
        else:
            for r, out in enumerate(outs):
                out[...] = grid[r * frames : (r + 1) * frames]

    key_place = lax.broadcasted_iota(jnp.int32, (rows, GROUP * rows), 0) % sub
    query_place = lax.broadcasted_iota(jnp.int32, (rows, GROUP * rows), 1) % sub
    bias = jnp.where(key_place == query_place, 0.0, -1e30)

    after_space = tokens(pieces)
    unit, rate = normalise(after_space)
    normed_time[...] = (unit * norm[2:3] + norm[3:4]).astype(BF)
    qkv[...] = dot(normed_time[...], qkv_w[...], NN).astype(BF)
    groups = width // WIDE
    for j in range(parts):
        at_rows = slice(j * rows, (j + 1) * rows)
        for g in range(groups):
            at = g * WIDE
            out, logsum = attend(
                qkv[at_rows, at : at + WIDE],
                qkv[at_rows, width + at : width + at + WIDE],
                qkv[at_rows, 2 * width + at : 2 * width + at + WIDE],
                bias,
            )
            mixed[at_rows, at : at + WIDE] = out
            probs_logsum[j * groups + g : j * groups + g + 1] = logsum
    after_time = after_space + dot(mixed[...], out_w[...], NT)
    unit2, rate2 = normalise(after_time)
    normed_mlp[...] = (unit2 * norm[4:5] + norm[5:6]).astype(BF)
    if joint:

        @pl.when(step == each)
        def _():
            late_copy(0).wait()
            for r in range(1, n_in):
                late_copy(r).wait_recv()
            cot_fetch(late, 0, slot).start()

        @pl.when(jnp.logical_and(step >= each, step + 1 < steps))
        def _():
            cot_fetch(late, step + 1 - each, 1 - slot).start()

        cot_fetch(cots[0], 0, slot).wait()
    cot = tokens([cot_in.at[slot]] if joint else cots)
    grad_result[...] = cot.astype(BF)
    result = after_time
    grad_normed = None
    for c in range(in_w.shape[0]):
        cols = slice(c * in_w.shape[2], (c + 1) * in_w.shape[2])
        pre = dot(normed_mlp[...], in_w[c], NN)
        below, density = gelu_parts(pre)
        hidden[:, cols] = (pre * below).astype(BF)
        result = result + dot(hidden[:, cols], unit_w[c], NT)
        grad_hidden = dot(grad_result[...], unit_w[c], NN)
        grad_pre[:, cols] = (grad_hidden * (below + pre * density)).astype(BF)
        term = dot(grad_pre[:, cols], in_w[c], NT)
        grad_normed = term if c == 0 else grad_normed + term
    scatter(result, results)

    @pl.when(pl.program_id(0) == 0)
    def _():
        norm_out[...] = jnp.zeros_like(norm_out)

    norm_out[2:3] += jnp.sum(grad_normed * unit2, axis=0, keepdims=True)
    norm_out[3:4] += jnp.sum(grad_normed, axis=0, keepdims=True)
    grad_after = cot + norm_back(grad_normed, norm[4:5], unit2, rate2)
    grad_time[...] = grad_after.astype(BF)
    grad_mixed = dot(grad_time[...], out_w[...], NN).astype(BF)
    for j in range(parts):
        at_rows = slice(j * rows, (j + 1) * rows)
        for g in range(groups):
            at = g * WIDE
            back = attend_back(
                qkv[at_rows, at : at + WIDE],
                qkv[at_rows, width + at : width + at + WIDE],
                qkv[at_rows, 2 * width + at : 2 * width + at + WIDE],
                grad_mixed[at_rows, at : at + WIDE],
                probs_logsum[j * groups + g : j * groups + g + 1],
                bias,
            )
            for i, part in enumerate(back):
                dqkv[at_rows, i * width + at : i * width + at + WIDE] = part
    store_columns(
        columns,
        [dqkv[:, i * width : (i + 1) * width] for i in range(3)] + [mixed[...]],
        n_parts,
    )
    grad_normed = dot(dqkv[...], qkv_w[...], NT)
    norm_out[0:1] += jnp.sum(grad_normed * unit, axis=0, keepdims=True)
    norm_out[1:2] += jnp.sum(grad_normed, axis=0, keepdims=True)
    grad_space = grad_after + norm_back(grad_normed, norm[2:3], unit, rate)
    if not joint:
        scatter(grad_space, grads)
        return
    scatter(grad_space, [outgoing.at[step]])
    received = grads[0]
    micros = received.shape[0]
    m, at = step // each, pl.multiple_of(lax.rem(step, each) * places, 8)
    for r in range(n_in):
        src, dst = outgoing.at[step, r], received.at[m, r, :, pl.ds(at, places)]
        if r == 0:
            pltpu.make_async_copy(src, dst, send.at[m, 0]).start()
        else:
            pltpu.make_async_remote_copy(
                src_ref=src, dst_ref=dst, send_sem=send.at[m, r], recv_sem=recv.at[m, r],
                device_id=to_z[r], device_id_type=MESH,
            ).start()

    @pl.when(step == steps - 1)
    def _():
        for r in range(1, n_in):
            late_copy(r).wait_send()
        for m in range(micros):
            for r in range(n_in):
                src = outgoing.at[pl.ds(m * each, each), r]
                dst = received.at[m, r]
                if r == 0:
                    pltpu.make_async_copy(dst, dst, send.at[m, 0]).wait()
                else:
                    for ref, wait in ((src, "wait_send"), (dst, "wait_recv")):
                        copy = pltpu.make_async_remote_copy(
                            src_ref=ref, dst_ref=ref, send_sem=send.at[m, r],
                            recv_sem=recv.at[m, r], device_id=to_z[r], device_id_type=MESH,
                        )
                        getattr(copy, wait)()


def time_layer(pieces, cots, qkv_w, out_w, in_w, unit_w, norm):
    joint = len(pieces) == 1
    frames, places, width = pieces[0].shape[-3:]
    n_in = pieces[0].shape[1] if joint else len(pieces)
    micros = pieces[0].shape[0] if joint else 1
    block = 16 if places % 16 == 0 else 8
    each = places // block
    sub = 8
    tokens = frames * n_in * block
    count = frames * n_in * places * micros
    hidden = in_w.shape[0] * in_w.shape[2]
    whole = pl.BlockSpec(memory_space=pltpu.VMEM)
    if joint:
        piece = pl.BlockSpec(
            (None, n_in, frames, block, width), lambda b: (b // each, 0, 0, b % each, 0)
        )
        any_spec = pl.BlockSpec(memory_space=pl.ANY)
        given = [piece, any_spec, any_spec]
        moved = [piece, any_spec, any_spec]
    else:
        piece = pl.BlockSpec((frames, block, width), lambda b: (0, b, 0))
        given = moved = [piece] * (2 * n_in)
    row = lambda cols: pl.BlockSpec((tokens, cols), lambda b: (b, 0))
    kept = [width, 4 * width, width, width, hidden, hidden, width]
    dma = pltpu.SemaphoreType.DMA
    sending = [
        pltpu.VMEM((micros * each, n_in, frames, block, width), BF),
        pltpu.VMEM((2, n_in, frames, block, width), BF),
        dma((micros, n_in)),
        dma((micros, n_in)),
        dma((n_in,)),
        dma((n_in,)),
        dma((2,)),
    ]
    sent = [jax.ShapeDtypeStruct(a.shape, BF) for a in pieces + cots]
    if joint:
        sent = [jax.ShapeDtypeStruct(a.shape, BF) for a in (pieces[0], pieces[0], cots[0])]
    return pl.pallas_call(
        partial(time_kernel, joint, n_in, in_w.shape[0], sub),
        grid=(micros * each,),
        in_specs=given + [whole] * 5,
        out_specs=moved + [row(cols) for cols in kept] + [pl.BlockSpec((4, width), lambda b: (0, 0))],
        out_shape=sent
        + [jax.ShapeDtypeStruct((count, cols), BF) for cols in kept]
        + [jax.ShapeDtypeStruct((4, width), F32)],
        scratch_shapes=[
            pltpu.VMEM((tokens, 3 * width), BF),
            pltpu.VMEM((tokens, 3 * width), BF),
            pltpu.VMEM((tokens, width), BF),
            pltpu.VMEM((8 * (block // sub), GROUP * frames * n_in * sub), F32),
        ]
        + (sending if joint else []),
        compiler_params=pltpu.CompilerParams(
            vmem_limit_bytes=60 * MIB,
            collective_id=4 if joint else None,
            has_side_effects=joint,
        ),
        cost_estimate=pl.CostEstimate(
            flops=2 * count * width * 2 * (4 * width + 2 * hidden),
            bytes_accessed=count * 26000,
            transcendentals=0,
        ),
    )(*pieces, *cots, qkv_w, out_w, in_w, unit_w, norm)


STEP = 192


class Copies:
    def __init__(self, send, recv):
        self.send, self.recv, self.count, self.all = send, recv, 0, []

    def add(self, src, dst, peer):
        copy = pltpu.make_async_remote_copy(
            src_ref=src, dst_ref=dst, send_sem=self.send.at[self.count],
            recv_sem=self.recv.at[self.count], device_id=peer, device_id_type=MESH,
        )
        self.count += 1
        self.all.append(copy)
        return copy


def start_all(copies):
    for copy in copies:
        copy.start()


def arrive(copies):
    for copy in copies:
        copy.wait_recv()


def blocks(count, body):
    lax.fori_loop(
        0, count // STEP, lambda i, _: body(pl.ds(pl.multiple_of(i * STEP, STEP), STEP)), None
    )


def back_kernel(
    results, grads, xs, qkv_in, mixed_in, logsum_in, qkv_w, out_w, norm_in,
    tail_time, rows_c, cols_c, rows_d, cols_d, rows_b, rows_b2, cols_b,
    out, tail_out, acts, input_grad, normed_a, low_a, cols_a, res_half,
    turned, stage, tile_in, sent, got1, held, got2, got3, total, got4,
    w_qkv, w_out, norm, logsum, dqkv, tail_sum, tail_got,
    stage_sem, tile_sem, frame_sem, out_sem, load_sem, send, recv, r_send, r_recv, i_send, i_recv,
):
    my_tp, my_y, my_z = lax.axis_index("tp"), lax.axis_index("clip"), lax.axis_index("fp")
    n_tp, n_z = lax.axis_size("tp"), lax.axis_size("fp")
    core, x = lax.rem(my_tp, 2), my_tp // 2
    micros, _, frames, chunk, width = results.shape
    places = chunk * n_z
    part = places // n_tp
    depth, cols = held.shape[2:]
    half, own = depth // 2, depth // (2 * n_z)
    all_rows = tile_in.shape[1]
    to_tp = [{"tp": my_tp ^ s} for s in range(n_tp)]
    to_core, to_x = to_tp[1], to_tp[2]
    to_y = {"clip": my_y ^ 1}
    to_z = [{"fp": my_z ^ r} for r in range(n_z)]
    peers = to_tp[1:] + to_z[1:] + [to_y]
    barrier = pltpu.get_barrier_semaphore()
    for peer in peers:
        pl.semaphore_signal(barrier, inc=1, device_id=peer, device_id_type=MESH)

    remote = Copies(send, recv)
    lefts = [[rows_c], [rows_d], [rows_b, rows_b2], [normed_a, low_a]]
    rights = [cols_c, cols_d, cols_b, cols_a]
    slots = [[0], [1], [2, 3], [0, 1]]
    place = [0, 1, 2, 0]
    lanes = [
        (0, 0, cols, True),
        (1, 0, cols, True),
        (2, 0, cols, True),
        (3, 0, cols // 2, True),
        (3, cols // 2, cols // 2, False),
    ]
    parts = [(1 - x) * 2 + 1 - core, x * 2 + 1 - core, (1 - x) * 2 + core, x * 2 + core]
    far_rows = pl.ds(pl.multiple_of((1 - my_y) * half, 16), half)
    near_rows = pl.ds(pl.multiple_of(my_y * half, 16), half)
    firsts = [
        [remote.add(sent.at[place[j], p], got1.at[j, p], to_core) for p in (0, 1)]
        for j in range(4)
    ]
    seconds, thirds, fourths = [], [], []
    for j, lo, count, y_first in lanes:
        at = pl.ds(lo, count)
        spot = held.at[place[j]]
        if y_first:
            seconds.append(
                [
                    remote.add(
                        spot.at[p, far_rows, at], got2.at[j, pl.ds(p * half, half), at], to_y
                    )
                    for p in (0, 1)
                ]
            )
            thirds.append(remote.add(spot.at[0, near_rows, at], got3.at[j, :, at], to_x))
        else:
            seconds.append([remote.add(spot.at[0, :, at], got2.at[j, :, at], to_x)])
            thirds.append(remote.add(spot.at[1, far_rows, at], got3.at[j, :, at], to_y))
        fourths.append(
            [
                remote.add(
                    total.at[j, pl.ds(pl.multiple_of((my_z ^ r) * own, 16), own), at],
                    got4.at[j, r - 1, :, at],
                    to_z[r],
                )
                for r in range(1, n_z)
            ]
        )
    tails = [
        remote.add(tail_sum.at[min(step, 3)], tail_got.at[step], peer)
        for step, peer in enumerate([to_core, to_y, to_x] + to_z[1:])
    ]
    res_z = [
        [
            remote.add(
                results.at[m, r],
                res_half.at[m, :, pl.ds(pl.multiple_of(my_z * chunk, 16), chunk)],
                to_z[r],
            )
            for r in range(1, n_z)
        ]
        for m in range(micros)
    ]
    res_tp = [
        [
            remote.add(
                res_half.at[m, :, pl.ds(s * part, part)], acts.at[m, my_tp], to_tp[s]
            )
            for s in range(1, n_tp)
        ]
        for m in range(micros)
    ]

    loads = [
        pltpu.make_async_copy(src, dst, load_sem.at[i])
        for i, (src, dst) in enumerate(
            [(qkv_w, w_qkv), (out_w, w_out), (norm_in, norm), (logsum_in, logsum)]
        )
    ]
    own_res = [
        pltpu.make_async_copy(
            results.at[m, 0],
            res_half.at[m, :, pl.ds(pl.multiple_of(my_z * chunk, 16), chunk)],
            load_sem.at[4 + m],
        )
        for m in range(micros)
    ]
    home_res = [
        pltpu.make_async_copy(
            res_half.at[m, :, pl.ds(0, part)], acts.at[m, my_tp], load_sem.at[4 + micros + m]
        )
        for m in range(micros)
    ]

    def fetch(index, tiles):
        j, p = tiles[index]
        return pltpu.make_async_copy(
            rights[j].at[:, pl.ds(pl.multiple_of(parts[p] * cols, 128), cols)],
            tile_in.at[index % 2],
            tile_sem.at[index % 2],
        )

    def fetch_left(index, todo):
        j, i, piece = todo[index]
        return pltpu.make_async_copy(
            lefts[j][i].at[pl.ds(piece * depth, depth)], stage.at[index % 2], stage_sem.at[index % 2]
        )

    def left_pieces(chunks):
        return [
            (j, i, piece)
            for j in chunks
            for i in range(len(lefts[j]))
            for piece in range(all_rows // depth)
        ]

    def turn(chunk, todo):
        for index, (j, i, piece) in enumerate(todo):
            if j == chunk:
                fetch_left(index, todo).wait()
                turned[slots[j][i], :, piece * depth : (piece + 1) * depth] = stage[index % 2].T
                if index + 2 < len(todo):
                    fetch_left(index + 2, todo).start()

    def product(index, tiles):
        j, p = tiles[index]
        fetch(index, tiles).wait()
        if index + 1 < len(tiles):
            fetch(index + 1, tiles).start()
        right = tile_in.at[index % 2]
        if p >= 2:
            firsts[j][p - 2].wait_recv()

        for lo in range(0, cols, WIDE):
            at = slice(lo, lo + WIDE)
            value = dot(turned[slots[j][0]], right[:, at], NN)
            if len(slots[j]) == 2 and lo + WIDE > 3 * cols // 4:
                other = dot(turned[slots[j][1]], right[:, at], NN)
                lane_index = lax.broadcasted_iota(jnp.int32, (depth, WIDE), 1) + lo
                value = jnp.where(lane_index >= 3 * cols // 4, other, value)
            if p < 2:
                sent[place[j], p, :, at] = value.astype(BF)
            else:
                value = value + got1[j, p - 2, :, at].astype(F32)
                held[place[j], p - 2, :, at] = value.astype(BF)

        if p < 2:
            firsts[j][p].start()
        else:
            for lane, (k, _, _, y_first) in enumerate(lanes):
                if k == j and (y_first or p == 2):
                    seconds[lane][p - 2].start()

    def after_second(lane):
        j, lo, count, y_first = lanes[lane]
        at = pl.ds(lo, count)
        spot = held.at[place[j]]
        if y_first:
            for p in (0, 1):
                seconds[lane][p].wait_recv()

                def body(rows, p=p):
                    mine = pl.ds(pl.multiple_of(rows.start + my_y * half, STEP), STEP)
                    there = pl.ds(pl.multiple_of(rows.start + p * half, STEP), STEP)
                    value = spot[p, mine, at].astype(F32) + got2[j, there, at].astype(F32)
                    spot[p, mine, at] = value.astype(BF)

                blocks(half, body)
                if p == 0:
                    thirds[lane].start()
        else:
            seconds[lane][0].wait_recv()

            def body(rows):
                value = spot[1, rows, at].astype(F32) + got2[j, rows, at].astype(F32)
                spot[1, rows, at] = value.astype(BF)

            blocks(depth, body)
            thirds[lane].start()

    def after_third(lane):
        j, lo, count, _ = lanes[lane]
        at = pl.ds(lo, count)
        thirds[lane].wait_recv()

        def body(rows):
            mine = pl.ds(pl.multiple_of(rows.start + my_y * half, STEP), STEP)
            value = held[place[j], 1, mine, at].astype(F32) + got3[j, rows, at].astype(F32)
            total[j, rows, at] = value.astype(BF)

        blocks(half, body)
        start_all(fourths[lane])

    def after_fourth(lane):
        j, lo, count, _ = lanes[lane]
        at = pl.ds(lo, count)
        value = total[j, pl.ds(pl.multiple_of(my_z * own, 16), own), at].astype(F32)
        for r in range(1, n_z):
            fourths[lane][r - 1].wait_recv()
            value = value + got4[j, r - 1, :, at].astype(F32)
        out[j, :, at] = value

    tiles = [(j, p) for j in range(3) for p in (0, 1)] + [(j, p) for j in range(3) for p in (2, 3)]
    todo = left_pieces([0, 1, 2])
    fetch_left(0, todo).start()
    fetch(0, tiles).start()
    fetch_left(1, todo).start()
    for copy in loads + own_res:
        copy.start()
    turn(0, todo)
    pl.semaphore_wait(barrier, len(peers))
    start_all(res_z[0] + res_z[1])
    for index in range(len(tiles)):
        product(index, tiles)
        if index in (1, 3):
            turn((index + 1) // 2, todo)

    for copy in loads:
        copy.wait()
    frame_total = micros * frames

    def frame_loads(f, slot):
        buf = tile_in.at[slot]
        m, at = f // frames, lax.rem(f, frames)
        pairs = [
            (xs.at[f], buf.at[pl.ds(0, places)]),
            (mixed_in.at[f], buf.at[pl.ds(places, places)]),
        ]
        pairs += [
            (
                qkv_in.at[f, :, pl.ds(i * width, width)],
                buf.at[pl.ds((2 + i) * places, places)],
            )
            for i in range(3)
        ]
        pairs += [
            (
                grads.at[m, r, at],
                buf.at[pl.ds(pl.multiple_of(5 * places + (my_z ^ r) * chunk, 16), chunk)],
            )
            for r in range(n_z)
        ]
        return [
            pltpu.make_async_copy(src, dst, frame_sem.at[slot, i])
            for i, (src, dst) in enumerate(pairs)
        ]

    def frame_stores(f, slot):
        rows = pl.ds(pl.multiple_of(f * places, 16), places)
        buf = turned.at[slot]
        pairs = [
            (
                buf.at[pl.ds(t * places, places), pl.ds(0, width)],
                cols_a.at[rows, pl.ds(t * cols, cols)],
            )
            for t in range(n_tp)
        ]
        pairs += [
            (buf.at[pl.ds(0, places), pl.ds(width, width)], normed_a.at[rows]),
            (buf.at[pl.ds(places, places), pl.ds(width, width)], low_a.at[rows]),
        ]
        return [
            pltpu.make_async_copy(src, dst, out_sem.at[slot, i])
            for i, (src, dst) in enumerate(pairs)
        ]

    grad = sent.at[1]
    for p in (0, 1):
        firsts[1][p].wait_send()
    tail_sum[...] = jnp.zeros_like(tail_sum)
    tail_sum[0, 2:6] = tail_time[...]
    start_all(frame_loads(0, 0))

    def frame(f, carry):
        slot = lax.rem(f, 2)

        @pl.when(f + 1 < frame_total)
        def _():
            start_all(frame_loads(f + 1, 1 - slot))

        @pl.when(f == 3)
        def _():
            after_second(0)

        @pl.when(f == 6)
        def _():
            after_second(1)

        @pl.when(f == 7)
        def _():
            after_third(0)

        for m in range(micros):

            @pl.when(f == 2 + 3 * m)
            def _(m=m):
                own_res[m].wait()
                arrive(res_z[m])
                start_all(res_tp[m])
                home_res[m].start()

        for copy in frame_loads(f, slot):
            copy.wait()

        @pl.when(f >= 2)
        def _():
            for copy in frame_stores(f - 2, slot):
                copy.wait()

        buf, keep = tile_in.at[slot], turned.at[slot]
        block = lambda i: slice(i * places, (i + 1) * places)
        unit, rate = normalise(buf[block(0)].astype(F32))
        keep[0:places, width : 2 * width] = (unit * norm[0:1] + norm[1:2]).astype(BF)
        low = buf[block(5)]
        keep[places : 2 * places, width : 2 * width] = low
        grad_mixed = dot(low, w_out[...], NN).astype(BF)
        for g in range(width // WIDE):
            at = slice(g * WIDE, (g + 1) * WIDE)
            back = attend_back(
                buf[block(2), at], buf[block(3), at], buf[block(4), at],
                grad_mixed[:, at], logsum[f, g : g + 1], None,
            )
            for i, value in enumerate(back):
                dqkv[:, i * width + g * WIDE : i * width + (g + 1) * WIDE] = value
        span = cols // 4
        for t in range(n_tp):
            for i in range(3):
                keep[block(t), i * span : (i + 1) * span] = dqkv[
                    :, i * width + t * span : i * width + (t + 1) * span
                ]
            keep[block(t), 3 * span : 4 * span] = buf[block(1), t * span : (t + 1) * span]
        start_all(frame_stores(f, slot))
        grad_normed = dot(dqkv[...], w_qkv[...], NT)
        tail_sum[0, 0:1] += jnp.sum(grad_normed * unit, axis=0, keepdims=True)
        tail_sum[0, 1:2] += jnp.sum(grad_normed, axis=0, keepdims=True)
        value = low.astype(F32) + norm_back(grad_normed, norm[0:1], unit, rate)
        m, at = f // frames, lax.rem(f, frames)
        grad[m, pl.ds(pl.multiple_of(at * places, 16), places), :] = value.astype(BF)
        for s in range(n_tp):
            src = grad.at[m, pl.ds(pl.multiple_of(at * places + s * part, 16), part)]
            dst = input_grad.at[m, my_tp, at]
            if s == 0:
                pltpu.make_async_copy(src, dst, i_send.at[0]).start()
            else:
                pltpu.make_async_remote_copy(
                    src_ref=src, dst_ref=dst, send_sem=i_send.at[s], recv_sem=i_recv.at[s],
                    device_id=to_tp[s], device_id_type=MESH,
                ).start()
        return carry

    lax.fori_loop(0, frame_total, frame, 0)
    for f in (frame_total - 2, frame_total - 1):
        for copy in frame_stores(f, f % 2):
            copy.wait()
    tails[0].start()

    for p in (0, 1):
        firsts[0][p].wait_send()
    last = [(3, p) for p in range(4)]
    todo = left_pieces([3])
    fetch_left(0, todo).start()
    fetch(0, last).start()
    fetch_left(1, todo).start()
    turn(3, todo)
    product(0, last)
    product(1, last)
    after_second(2)
    after_third(1)
    tails[0].wait_recv()
    tail_sum[1] = tail_sum[0] + tail_got[0]
    tails[1].start()
    for p in (0, 1):
        seconds[0][p].wait_send()
    thirds[0].wait_send()
    product(2, last)
    product(3, last)
    after_fourth(0)
    tails[1].wait_recv()
    tail_sum[2] = tail_sum[1] + tail_got[1]
    tails[2].start()
    after_third(2)
    after_second(3)
    after_second(4)
    after_fourth(1)
    tails[2].wait_recv()
    tail_sum[3] = tail_sum[2] + tail_got[2]
    start_all(tails[3:])
    after_third(3)
    after_third(4)
    after_fourth(2)
    value = tail_sum[3]
    for r in range(n_z - 1):
        tails[3 + r].wait_recv()
        value = value + tail_got[3 + r]
    tail_out[...] = value
    after_fourth(3)
    after_fourth(4)
    for m in range(micros):
        arrive(res_tp[m])
        home_res[m].wait()
    for s in range(n_tp):
        dst = input_grad.at[:, my_tp ^ s]
        if s == 0:
            pltpu.make_async_copy(dst, dst, i_send.at[0]).wait()
        else:
            for ref, wait in ((dst, "wait_send"), (dst, "wait_recv")):
                copy = pltpu.make_async_remote_copy(
                    src_ref=ref, dst_ref=ref, send_sem=i_send.at[s], recv_sem=i_recv.at[s],
                    device_id=to_tp[s], device_id_type=MESH,
                )
                getattr(copy, wait)()
    done = firsts[0] + firsts[1] + seconds[0] + [thirds[0]]
    for copy in remote.all:
        if not any(copy is other for other in done):
            copy.wait_send()


def back(results, grads, xs, qkv, mixed, logsum, qkv_w, out_w, norm, tail_time, kept):
    normed_time, columns, grad_time, normed_mlp, grad_pre, hidden, grad_result = kept
    micros, n_z, frames, chunk, width = results.shape
    n_tp = lax.axis_size("tp")
    places = chunk * n_z
    total = micros * frames
    rows = total * places
    depth, cols = width, columns.shape[1] // n_tp
    half, own = depth // 2, depth // (2 * n_z)
    part = places // n_tp
    any_spec = pl.BlockSpec(memory_space=pl.ANY)
    vmem = pl.BlockSpec(memory_space=pltpu.VMEM)
    dma = pltpu.SemaphoreType.DMA
    shape = jax.ShapeDtypeStruct
    home = shape((micros, n_tp, frames, part, width), BF)
    return pl.pallas_call(
        back_kernel,
        in_specs=[any_spec] * 9 + [vmem] + [any_spec] * 7,
        out_specs=[vmem] * 2 + [any_spec] * 6,
        out_shape=[
            shape((4, own, cols), F32),
            shape((8, width), F32),
            home,
            home,
            shape((rows, width), BF),
            shape((rows, width), BF),
            shape((rows, n_tp * cols), BF),
            shape((micros, frames, places, width), BF),
        ],
        scratch_shapes=[
            pltpu.VMEM((4, depth, rows), BF),
            pltpu.VMEM((2, depth, width), BF),
            pltpu.VMEM((2, rows, cols), BF),
            pltpu.VMEM((3, 2, depth, cols), BF),
            pltpu.VMEM((4, 2, depth, cols), BF),
            pltpu.VMEM((3, 2, depth, cols), BF),
            pltpu.VMEM((4, depth, cols), BF),
            pltpu.VMEM((4, half, cols), BF),
            pltpu.VMEM((4, half, cols), BF),
            pltpu.VMEM((4, n_z - 1, own, cols), BF),
            pltpu.VMEM((width, 3 * width), BF),
            pltpu.VMEM((width, width), BF),
            pltpu.VMEM((8, width), F32),
            pltpu.VMEM(logsum.shape, F32),
            pltpu.VMEM((places, 3 * width), BF),
            pltpu.VMEM((4, 8, width), F32),
            pltpu.VMEM((2 + n_z, 8, width), F32),
            dma((2,)),
            dma((2,)),
            dma((2, 5 + n_z)),
            dma((2, n_tp + 2)),
            dma((4 + 2 * micros,)),
            dma((N_REMOTE,)),
            dma((N_REMOTE,)),
            dma((1,)),
            dma((1,)),
            dma((n_tp,)),
            dma((n_tp,)),
        ],
        compiler_params=pltpu.CompilerParams(
            vmem_limit_bytes=60 * MIB, collective_id=5, has_side_effects=True
        ),
        cost_estimate=pl.CostEstimate(
            flops=2 * rows * width * 23 * width,
            bytes_accessed=rows * width * 60,
            transcendentals=0,
        ),
    )(
        results, grads, xs, qkv, mixed, logsum, qkv_w, out_w, norm, tail_time,
        normed_mlp, grad_pre, grad_result, hidden, normed_time, grad_time, columns,
    )


N_REMOTE = 96
N_LOCAL = 24


def front_kernel(
    inputs, cot, shard, ln_shard,
    xs_out, time_in, cots, cot_late, qkv_out, mixed_out, logsum_out,
    qkv_a, out_a, qkv_b, out_b, in_w, unit_w, norms,
    xs, sent, raw, std_qkv, std_out, ln, cot_half, qkv, mixed,
    send, recv, t_send, t_recv, local,
):
    my_tp, my_y, my_z = lax.axis_index("tp"), lax.axis_index("clip"), lax.axis_index("fp")
    n_tp, n_z = lax.axis_size("tp"), lax.axis_size("fp")
    micros, _, frames, part, width = inputs.shape
    places = part * n_tp
    chunk = places // n_z
    own = shard.shape[1]
    half = n_z * own
    cols = shard.shape[2]
    to_tp = [{"tp": my_tp ^ s} for s in range(n_tp)]
    to_core, to_x = to_tp[1], to_tp[2]
    to_y = {"clip": my_y ^ 1}
    to_z = [{"fp": my_z ^ r} for r in range(n_z)]
    peers = to_tp[1:] + to_z[1:] + [to_y]
    barrier = pltpu.get_barrier_semaphore()
    for peer in peers:
        pl.semaphore_signal(barrier, inc=1, device_id=peer, device_id_type=MESH)

    remote = Copies(send, recv)
    locals_ = []

    def here(src, dst):
        copy = pltpu.make_async_copy(src, dst, local.at[len(locals_)])
        locals_.append(copy)
        copy.start()
        return copy

    tiles = [raw.at[0], raw.at[1], in_w, unit_w]
    mine = pl.multiple_of(my_y * half + my_z * own, 16)
    near = pl.multiple_of(my_y * half, 16)
    far = pl.multiple_of((1 - my_y) * half, 16)
    away = my_tp ^ 2
    cuts = [cols // 2] + [5 * cols // 6] * 3
    own_shards = []
    by_z, by_x, by_y, by_y2, by_x2, by_core = [], [], [], [], [], []
    for j, tile in enumerate(tiles):
        cut = cuts[j]
        one, two = pl.ds(0, cut), pl.ds(cut, cols - cut)
        own_rows, near_rows, far_rows = pl.ds(mine, own), pl.ds(near, half), pl.ds(far, half)

        def same(peer, *index, tile=tile):
            return remote.add(tile.at[index], tile.at[index], peer)

        by_z.append(
            [
                remote.add(shard.at[j], tile.at[my_tp, own_rows], to_z[r])
                for r in range(1, n_z)
            ]
        )
        by_x.append(same(to_x, my_tp, near_rows, one))
        by_y.append([same(to_y, my_tp, near_rows, one), same(to_y, away, near_rows, one)])
        by_core.append(
            [
                same(to_core, my_tp, near_rows),
                same(to_core, away, near_rows, one),
                same(to_core, my_tp, far_rows, one),
                same(to_core, away, far_rows, one),
            ]
        )
        if cut < cols:
            by_y2.append(same(to_y, my_tp, near_rows, two))
            by_x2.append(same(to_x, my_tp, slice(None), two))
            by_core[j] += [
                same(to_core, my_tp, far_rows, two),
                same(to_core, away, slice(None), two),
            ]
    ln_z = [
        remote.add(ln_shard, ln.at[pl.ds(mine, own)], to_z[r]) for r in range(1, n_z)
    ]
    ln_y = remote.add(ln.at[pl.ds(near, half)], ln.at[pl.ds(near, half)], to_y)
    x_in = [
        [
            remote.add(
                inputs.at[m, my_tp ^ s],
                xs.at[pl.ds(m * frames, frames), pl.ds(s * part, part)],
                to_tp[s],
            )
            for s in range(1, n_tp)
        ]
        for m in range(micros)
    ]
    cot_in = [
        [
            remote.add(cot.at[m, my_tp ^ s], half.at[:, pl.ds(s * part, part)], to_tp[s])
            for s in range(1, n_tp)
        ]
        for m, half in enumerate((cot_half, cot_late))
    ]
    cot_z = [
        remote.add(
            cot_half.at[:, pl.ds(pl.multiple_of((my_z ^ r) * chunk, 16), chunk)],
            cots.at[r],
            to_z[r],
        )
        for r in range(1, n_z)
    ]

    own_x = [
        here(inputs.at[m, my_tp], xs.at[pl.ds(m * frames, frames), pl.ds(0, part)])
        for m in range(micros)
    ]
    own_cot = [
        here(cot.at[m, my_tp], half.at[:, pl.ds(0, part)])
        for m, half in enumerate((cot_half, cot_late))
    ]
    own_w = [here(shard.at[j], tile.at[my_tp, pl.ds(mine, own)]) for j, tile in enumerate(tiles)]
    own_ln = here(ln_shard, ln.at[pl.ds(mine, own)])

    pl.semaphore_wait(barrier, len(peers))
    start_all(by_z[0] + ln_z + x_in[0])

    def gather_start(j):
        own_w[j].wait()
        arrive(by_z[j])
        by_x[j].start()
        by_y2[j].start()
        by_core[j][0].start()

    def gather_first(j):
        by_x[j].wait_recv()
        start_all(by_y[j])
        by_core[j][1].start()

    def gather_second(j):
        by_y2[j].wait_recv()
        by_x2[j].start()
        by_core[j][4].start()

    def gather_last(j):
        arrive(by_y[j])
        start_all(by_core[j][2:4])
        by_x2[j].wait_recv()
        by_core[j][5].start()

    def standard(j):
        span = cols // 4
        for t in range(n_tp):
            for i in range(3):
                std_qkv[j, :, i * width + t * span : i * width + (t + 1) * span] = raw[
                    j, t, :, i * span : (i + 1) * span
                ]
            std_out[j, :, t * span : (t + 1) * span] = raw[j, t, :, 3 * span : 4 * span]

    gather_start(0)
    start_all(by_z[1] + by_z[2] + by_z[3])
    own_ln.wait()
    arrive(ln_z)
    ln_y.start()
    gather_first(0)
    gather_second(0)
    gather_start(1)
    start_all(cot_in[0] + x_in[1])
    gather_last(0)
    ln_y.wait_recv()
    norms[...] = ln[...].astype(F32).T[: norms.shape[0]]
    gather_start(2)
    gather_start(3)
    arrive(by_core[0])
    standard(0)
    gather_second(1)
    gather_first(1)
    own_x[0].wait()
    arrive(x_in[0])
    weights_out = [here(std_qkv.at[0], qkv_a), here(std_out.at[0], out_a)]

    def frame(f, carry):
        @pl.when(f == 2)
        def _():
            own_cot[0].wait()
            arrive(cot_in[0])
            start_all(cot_z)
            gather_second(2)
            gather_second(3)

        @pl.when(f == frames)
        def _():
            own_x[1].wait()
            arrive(x_in[1])
            gather_first(2)

        @pl.when(f == frames + 2)
        def _():
            gather_first(3)
            start_all(cot_in[1])

        x = xs[f].astype(F32)
        unit, _ = normalise(x)
        normed = (unit * norms[0:1] + norms[1:2]).astype(BF)
        qkv[f] = dot(normed, std_qkv[0], NN).astype(BF)
        for g in range(width // WIDE):
            at = g * WIDE
            out, logsum = attend(
                qkv[f, :, at : at + WIDE],
                qkv[f, :, width + at : width + at + WIDE],
                qkv[f, :, 2 * width + at : 2 * width + at + WIDE],
                None,
            )
            mixed[f, :, at : at + WIDE] = out
            logsum_out[f, g : g + 1] = logsum
        sent[f] = (x + dot(mixed[f], std_out[0], NT)).astype(BF)
        m, at_frame = f // frames, lax.rem(f, frames)
        for r in range(n_z):
            src = sent.at[f, pl.ds(pl.multiple_of((my_z ^ r) * chunk, 16), chunk)]
            dst = time_in.at[m, r, at_frame]
            if r == 0:
                pltpu.make_async_copy(src, dst, t_send.at[m, 0]).start()
            else:
                pltpu.make_async_remote_copy(
                    src_ref=src, dst_ref=dst, send_sem=t_send.at[m, r],
                    recv_sem=t_recv.at[m, r], device_id=to_z[r], device_id_type=MESH,
                ).start()
        return carry

    lax.fori_loop(0, micros * frames, frame, 0)
    kept = [here(xs, xs_out), here(qkv, qkv_out), here(mixed, mixed_out)]
    gather_last(1)
    arrive(by_core[1])
    standard(1)
    weights_out += [here(std_qkv.at[1], qkv_b), here(std_out.at[1], out_b)]
    own_cots = [
        here(cot_half.at[:, pl.ds(pl.multiple_of(my_z * chunk, 16), chunk)], cots.at[0])
    ]
    gather_last(2)
    gather_last(3)
    arrive(by_core[2])
    arrive(by_core[3])
    own_cot[1].wait()
    arrive(cot_in[1])
    arrive(cot_z)
    for m in range(micros):
        for r in range(n_z):
            src = sent.at[
                pl.ds(m * frames, frames), pl.ds(pl.multiple_of((my_z ^ r) * chunk, 16), chunk)
            ]
            dst = time_in.at[m, r]
            if r == 0:
                pltpu.make_async_copy(src, dst, t_send.at[m, 0]).wait()
            else:
                pltpu.make_async_remote_copy(
                    src_ref=src, dst_ref=dst, send_sem=t_send.at[m, r],
                    recv_sem=t_recv.at[m, r], device_id=to_z[r], device_id_type=MESH,
                ).wait()
    for copy in remote.all:
        copy.wait_send()
    for copy in kept + weights_out + own_cots:
        copy.wait()


def front(inputs, cot, shard, ln_shard):
    micros, clips, frames, part, width = inputs.shape
    n_tp, n_z = lax.axis_size("tp"), lax.axis_size("fp")
    places = part * n_tp
    total = micros * frames
    chunk = places // n_z
    cols = shard.shape[2]
    groups = width // WIDE
    any_spec = pl.BlockSpec(memory_space=pl.ANY)
    vmem = pl.BlockSpec(memory_space=pltpu.VMEM)
    dma = pltpu.SemaphoreType.DMA
    shape = jax.ShapeDtypeStruct
    weights = [(width, 3 * width), (width, width)] * 2 + [(n_tp, width, cols)] * 2
    return pl.pallas_call(
        front_kernel,
        in_specs=[any_spec] * 4,
        out_specs=[any_spec] * 6 + [vmem] + [any_spec] * 6 + [vmem],
        out_shape=[
            shape((total, places, width), BF),
            shape((micros, n_z, frames, chunk, width), BF),
            shape((n_z, frames, chunk, width), BF),
            shape((frames, places, width), BF),
            shape((total, places, 3 * width), BF),
            shape((total, places, width), BF),
            shape((total, groups, GROUP * places), F32),
        ]
        + [shape(dims, BF) for dims in weights]
        + [shape((8, width), F32)],
        scratch_shapes=[
            pltpu.VMEM((total, places, width), BF),
            pltpu.VMEM((total, places, width), BF),
            pltpu.VMEM((2, n_tp, width, cols), BF),
            pltpu.VMEM((2, width, 3 * width), BF),
            pltpu.VMEM((2, width, width), BF),
            pltpu.VMEM((width, ln_shard.shape[1]), BF),
            pltpu.VMEM((frames, places, width), BF),
            pltpu.VMEM((total, places, 3 * width), BF),
            pltpu.VMEM((total, places, width), BF),
            dma((N_REMOTE,)),
            dma((N_REMOTE,)),
            dma((micros, n_z)),
            dma((micros, n_z)),
            dma((N_LOCAL,)),
        ],
        compiler_params=pltpu.CompilerParams(
            vmem_limit_bytes=60 * MIB, collective_id=3, has_side_effects=True
        ),
        cost_estimate=pl.CostEstimate(
            flops=2 * total * places * width * 5 * width,
            bytes_accessed=total * places * width * 16,
            transcendentals=0,
        ),
    )(inputs, cot, shard, ln_shard)


def to_peer(value, axis, step):
    n = lax.axis_size(axis)
    return lax.ppermute(value, axis, [(i, i ^ step) for i in range(n)])


def swap(pieces, axis):
    return [piece if s == 0 else to_peer(piece, axis, s) for s, piece in enumerate(pieces)]


def pick(stack, index):
    return lax.dynamic_index_in_dim(stack, index, 0, keepdims=False)


def shards(
    inputs, cotangent, qkv_weight, out_spatial, out_temporal, mlp_in, mlp_out, ln_gain, ln_bias
):
    micros, clips, frames, local, width = inputs.shape
    n_tp, n_fp = lax.axis_size("tp"), lax.axis_size("fp")
    n_cf = lax.axis_size("clip") * n_fp
    assert clips == n_tp
    my_tp, my_fp = lax.axis_index("tp"), lax.axis_index("fp")
    depth = qkv_weight.shape[2]
    span = qkv_weight.shape[3]
    places = n_tp * local
    chunk = places // n_fp
    at = my_fp.astype(jnp.int32)[None]

    first = jnp.concatenate([qkv_weight[0, i] for i in range(3)] + [out_spatial.T], axis=1)
    second = jnp.concatenate([qkv_weight[1, i] for i in range(3)] + [out_temporal.T], axis=1)
    axes = ("clip", "fp", "tp")
    ln_rows = [v[i] for i in range(3) for v in (ln_gain, ln_bias)]
    whole_rows = depth % 16 == 0 and n_tp == 4 and lax.axis_size("clip") == 2 and micros == 2
    whole_rows = whole_rows and frames * places == width and span * 4 == width

    def from_chunks(chunks):
        stack = jnp.stack(chunks)
        joined = jnp.concatenate([pick(stack, my_fp ^ c) for c in range(n_fp)], axis=1)
        return [joined[:, s * local : (s + 1) * local] for s in range(n_tp)]

    def outward(pieces):
        stack = jnp.stack(swap(pieces, "tp"))
        return jnp.stack([pick(stack, my_tp ^ c) for c in range(n_tp)])

    mine = lax.axis_index("clip") * n_fp + my_fp
    kinds = lambda v: [v[:, i * span : (i + 1) * span] for i in range(4)]

    def arranged(acts, grad_input, late, space, norm_grads):
        norm_grads = norm_grads[:6].reshape(3, 2, n_cf, depth)
        norm_grads = lax.dynamic_index_in_dim(norm_grads, mine, 2, keepdims=False)
        space_g, time_g = kinds(space), kinds(late[2])
        return (
            acts,
            grad_input,
            jnp.stack([jnp.stack(space_g[:3]), jnp.stack(time_g[:3])]),
            space_g[3].T,
            time_g[3].T,
            late[0],
            late[1].T,
            norm_grads[:, 0],
            norm_grads[:, 1],
        )

    if whole_rows:
        ln_shard = jnp.stack(ln_rows + [jnp.zeros_like(ln_rows[0])] * 122, axis=1)
        shard = jnp.stack([first, second, mlp_in, mlp_out.T])
        (
            xs, time_pieces, cots, cot_late, qkv, mixed, logsum,
            qkv_space_w, out_space_w, qkv_time_w, out_time_w, in_w, unit_w, norms,
        ) = front(inputs, cotangent, shard, ln_shard)
        results, grads, _, *kept, tail = time_layer(
            [time_pieces], [cots, cot_late], qkv_time_w, out_time_w, in_w, unit_w, norms
        )
        sums, norm_grads, acts, input_grad, *_ = back(
            results, grads, xs, qkv, mixed, logsum, qkv_space_w, out_space_w, norms, tail, kept
        )
        return arranged(acts, input_grad.astype(F32), sums, sums[3], norm_grads)

    def gathered(part):
        return lax.all_gather(part, axes).reshape(n_cf, n_tp, depth, part.shape[1])

    def attention_weights(raw):
        raw = raw.reshape(n_cf, n_tp, depth, 4, span).transpose(3, 0, 2, 1, 4)
        raw = raw.reshape(4, n_cf * depth, n_tp * span)
        return jnp.concatenate([raw[0], raw[1], raw[2]], axis=1), raw[3]

    def unit_weights(raw):
        return raw.transpose(1, 0, 2, 3).reshape(n_tp, n_cf * depth, raw.shape[3])

    norms = lax.all_gather(jnp.stack(ln_rows), ("clip", "fp"))
    norms = norms.transpose(1, 0, 2).reshape(6, n_cf * depth).astype(F32)
    qkv_space_w, out_space_w = attention_weights(gathered(first))
    rest = gathered(jnp.concatenate([second, mlp_in, mlp_out.T], axis=1))
    qkv_time_w, out_time_w = attention_weights(rest[..., : 4 * span])
    in_w = unit_weights(rest[..., 4 * span : 4 * span + mlp_in.shape[1]])
    unit_w = unit_weights(rest[..., 4 * span + mlp_in.shape[1] :])

    def inward(array, m):
        return swap([pick(array[m], my_tp ^ s) for s in range(n_tp)], "tp")

    def to_chunks(pieces):
        joined = jnp.concatenate(pieces, axis=1)
        return [
            lax.dynamic_slice_in_dim(joined, (my_fp ^ r) * chunk, chunk, 1)
            for r in range(n_fp)
        ]

    space_kept, time_given = [], []
    for m in range(micros):
        x = inward(inputs, m)
        cots = swap(to_chunks(inward(cotangent, m)), "fp")
        out = space_forward(x, qkv_space_w, out_space_w, norms, at, n_fp)
        time_given.append((swap(out[:n_fp], "fp"), cots))
        space_kept.append((x,) + tuple(out[n_fp:]) + (0,))
    time_kept = []
    results = []
    space_grads = []
    for m in range(micros):
        pieces, cots = time_given[m]
        out = time_layer(pieces, cots, qkv_time_w, out_time_w, in_w, unit_w, norms)
        results.append(outward(from_chunks(swap(out[:n_fp], "fp"))))
        space_grads.append(swap(out[n_fp : 2 * n_fp], "fp"))
        time_kept.append(out[2 * n_fp :])
    space_rows = []
    input_grads = []
    flat = lambda v: v.reshape(-1, v.shape[-1])
    kept = lambda i: [k[i] for k in time_kept]
    time_chunks = [
        ([kept(3)], kept(4), True),
        ([kept(6)], kept(5), False),
        ([kept(0), kept(2)], kept(1), True),
    ]
    for m in range(micros):
        x, qkv, mixed, logsum, skip = space_kept[m]
        out = space_backward(
            x, space_grads[m], qkv, mixed, logsum, qkv_space_w, out_space_w, norms, at, skip, n_tp
        )
        input_grads.append(outward(out[:n_tp]).astype(F32))
        normed, low, columns, norm_grad = out[n_tp:]
        space_rows.append((flat(normed), flat(low), flat(columns), norm_grad))
    rows = lambda i: [k[i] for k in space_rows]
    space_chunk = ([rows(0), rows(1)], rows(2), True)
    early = scatter_grads([space_chunk], n_cf, n_tp)
    late = scatter_grads(time_chunks, n_cf, n_tp)
    norm_grads = lax.psum(jnp.concatenate([sum(rows(3)), sum(kept(7))]), axes)
    return arranged(jnp.stack(results), jnp.stack(input_grads), late, early[0], norm_grads)


def scatter_grads(chunks, n_cf, n_tp):
    tiles = []
    for lefts, rights, _ in chunks:
        cols = rights[0].shape[1] // n_tp
        total = sum(dot(a, b, TN) for a, b in zip(lefts[0], rights))
        total = total.reshape(total.shape[0], n_tp, cols)
        if len(lefts) == 2:
            other = sum(dot(a, b, TN) for a, b in zip(lefts[1], rights))
            other = other.reshape(other.shape[0], n_tp, cols)
            at = 3 * cols // 4
            total = jnp.concatenate([total[..., :at], other[..., at:]], axis=2)
        total = total.reshape(n_cf, total.shape[0] // n_cf, n_tp, cols).transpose(0, 2, 1, 3)
        tiles.append(total.reshape((n_cf * n_tp,) + total.shape[2:]))
    return lax.psum_scatter(jnp.stack(tiles, 1), ("clip", "fp", "tp"), scatter_dimension=0)


def solution(mesh):
    spread = P(None, "clip", "fp", "tp", None)
    return jax.shard_map(
        shards,
        mesh=mesh,
        in_specs=(
            spread,
            spread,
            P(None, None, ("clip", "fp"), "tp"),
            P("tp", ("clip", "fp")),
            P("tp", ("clip", "fp")),
            P(("clip", "fp"), "tp"),
            P("tp", ("clip", "fp")),
            P(None, ("clip", "fp")),
            P(None, ("clip", "fp")),
        ),
        out_specs=(
            spread,
            spread,
            P(None, None, ("clip", "fp"), "tp"),
            P("tp", ("clip", "fp")),
            P("tp", ("clip", "fp")),
            P(("clip", "fp"), "tp"),
            P("tp", ("clip", "fp")),
            P(None, ("clip", "fp")),
            P(None, ("clip", "fp")),
        ),
        check_vma=False,
    )
```

profile of v0, /device:TPU:0, one launch (start us, length us, event | category | flops | bytes accessed | tf_op | source)
XLA Modules:
  0.0 446.0 jit_solution(14380361111285143899)
XLA Ops:
  0.6 0.0 copy-start.3
  0.7 0.0 copy-start.4
  0.7 0.9 slice_bitcast_fusion.17
  1.6 0.9 copy.18
  2.5 0.9 copy.19
  3.4 0.1 maximum_bitcast_fusion.2
  3.5 1.9 pad_maximum_fusion.shard
  5.4 0.0 copy-done.3
  5.4 0.1 copy.20
  5.6 0.0 copy-done.4
  5.6 0.1 copy.21
  5.7 0.1 copy.22
  5.8 0.1 copy.23
  5.9 0.1 copy.24
  6.1 0.1 copy.25
  6.3 0.8 stack.76.ln_shard
  7.0 139.8 %shard_map.160 = (bf16[8,192,768]{2,1,0:T(8,128)(2,1)}, bf16[2,4,4,48,768]{4,3,2,1,0:T(8,128)(2,1)}, bf16[4,4,48,768]{3,2,1,0:T(8,128)(2,1)}, bf16[4,192,768]{2,...) custom-call(bf16[2,4,4,48,768]{4,3,2,1,0:T(8,128)(2,1)} %inputs.1, ...), custom_call_target="tpu_custom_call" | custom-call | flops 9059696640 | bytes 18874368 | tf_op jit(solution)/shard_map/pallas_call | solution.py:1356
  146.9 117.4 %shard_map.161 = (bf16[2,4,4,48,768]{4,3,2,1,0:T(8,128)(2,1)}, bf16[2,4,4,48,768]{4,3,2,1,0:T(8,128)(2,1)}, bf16[4,4,48,768]{3,2,1,0:T(8,128)(2,1)}, bf16[1536,7...) custom-call(bf16[2,4,4,48,768]{4,3,2,1,0:T(8,128)(2,1)} %get-tuple-e, ...), custom_call_target="tpu_custom_call" | custom-call | flops 43486543872 | bytes 39936000 | tf_op jit(solution)/shard_map/pallas_call | solution.py:510
  264.2 171.2 %shard_map.162 = (f32[4,96,768]{2,1,0:T(8,128)}, f32[8,768]{1,0:T(8,128)}, bf16[2,4,4,48,768]{4,3,2,1,0:T(8,128)(2,1)}, bf16[2,4,4,48,768]{4,3,2,1,0:T(8,128)(2,...) custom-call(bf16[2,4,4,48,768]{4,3,2,1,0:T(8,128)(2,1)} %get-tuple-e, ...), custom_call_target="tpu_custom_call" | custom-call | flops 41674604544 | bytes 70778880 | tf_op jit(solution)/shard_map/pallas_call | solution.py:1027
  435.4 2.1 slice_bitcast_fusion
  437.5 0.0 copy-start
  437.5 0.1 slice_bitcast_fusion.5
  437.7 0.1 slice_bitcast_fusion.4
  437.8 0.9 pad_maximum_fusion.1
  438.7 0.7 copy-done
  439.4 0.0 copy-start.2
  439.4 0.0 copy-start.1
  439.4 2.8 convert_element_type.3
  442.2 0.7 copy.27
  442.9 0.7 copy.28
  443.6 0.0 copy-done.2
  443.6 0.1 reshape.21
  443.7 0.6 slice_bitcast_fusion.18
  444.3 0.0 copy-done.1
  444.3 1.4 copy.32
  (11 shorter events, 0.1 us)
Async XLA Ops:
  0.6 4.8 %copy-start.3 = (bf16[3,96]{1,0:T(4,128)(2,1)S(1)}, bf16[3,96]{1,0:T(4,128)(2,1)}, u32[]{:S(2)}) copy-start(bf16[3,96]{1,0:T(4,128)(2,1)} %param.16) | copy-start | bytes 1732
  0.7 4.9 %copy-start.4 = (bf16[3,96]{1,0:T(4,128)(2,1)S(1)}, bf16[3,96]{1,0:T(4,128)(2,1)}, u32[]{:S(2)}) copy-start(bf16[3,96]{1,0:T(4,128)(2,1)} %param.17) | copy-start | bytes 1732
  437.5 1.9 copy-start
  439.4 4.3 copy-start.2
  439.4 4.9 %copy-start.1 = (bf16[2,4,4,48,768]{4,3,2,1,0:T(8,128)(2,1)S(1)}, bf16[2,4,4,48,768]{4,3,2,1,0:T(8,128)(2,1)}, u32[]{:S(2)}) copy-start(bf16[2,4,4,48,768]{4,3,2,1,0:T(8,128)(2,1)} %get-tuple-element.111) | copy-start | bytes 7077892
where the time goes:
time: 451 us; the launch traced here: 446 us
  Pallas kernels  428 us (95%)
  local copies, waits for them, and re-layouts  10.9 us (2%)
  other arithmetic  5.68 us (1%)
    pallas_call x1, Pallas kernels, back(): pl.pallas_call(back_kernel, in_specs=[any_spec] * 9 + [vmem] + [any_spec]...  171 us
    pallas_call x1, Pallas kernels, front(): pl.pallas_call(front_kernel, in_specs=[any_spec] * 4, out_specs=[any_spec...  140 us
    pallas_call x1, Pallas kernels, time_layer(): pl.pallas_call(partial(time_kernel, joint, n_in, in_w.shape[0], sub), gri...  117 us

commit v1 on v0

--- a/solution.py
+++ b/solution.py
@@ -275,50 +275,129 @@
         hidden,
         grad_result,
         norm_out,
-        qkv,
+        qkv_all,
         dqkv,
-        mixed,
-        probs_logsum,
-    ) = rest[:12]
+        mixed_all,
+        logsum_all,
+        after_all,
+    ) = rest[:13]
     if joint:
-        step, steps = pl.program_id(0), pl.num_programs(0)
-        outgoing, cot_in, send, recv, c_send, c_recv, cot_sem = rest[12:]
+        (
+            outgoing, cot_in, in_held, unit_held, send, recv, c_send, c_recv, cot_sem,
+            g_send, g_recv, w_sem,
+        ) = rest[13:]
         late = grads[1]
-        my_z = lax.axis_index("fp")
+        my_tp, my_y, my_z = lax.axis_index("tp"), lax.axis_index("clip"), lax.axis_index("fp")
         to_z = [{"fp": my_z ^ r} for r in range(n_in)]
+        to_core, to_x, to_y = {"tp": my_tp ^ 1}, {"tp": my_tp ^ 2}, {"clip": my_y ^ 1}
         block = results[0].shape[-2]
-        chunk = late.shape[2]
+        chunk = late.shape[3]
         each = chunk // block
-        slot = lax.rem(step, 2)
-
-        def late_copy(r):
-            src = cots[1].at[:, pl.ds(pl.multiple_of((my_z ^ r) * chunk, 16), chunk)]
+        steps = pl.num_programs(0)
+        count = steps // 2
+        step = pl.program_id(0)
+        at_block = lax.rem(step, count)
+        slot = lax.rem(at_block, 2)
+        half, cols = in_w.shape[1] // 2, in_w.shape[2]
+        near = pl.ds(pl.multiple_of(my_y * half, 16), half)
+        far = pl.ds(pl.multiple_of((1 - my_y) * half, 16), half)
+        one, two = pl.ds(0, cols // 2), pl.ds(cols // 2, cols // 2)
+        away = my_tp ^ 2
+        ways = [(in_w, in_held), (unit_w, unit_held)]
+
+        def gather(j, i):
+            given, held = ways[j]
+            src, at, peer = [
+                (given, (my_tp, near, one), to_y),
+                (given, (away, near, one), to_y),
+                (given, (my_tp, slice(None), two), to_x),
+                (given, (my_tp, near), to_core),
+                (given, (away, near, one), to_core),
+                (given, (my_tp, far, two), to_core),
+                (held, (my_tp, far, one), to_core),
+                (held, (away, far, one), to_core),
+                (held, (away, slice(None), two), to_core),
+            ][i]
+            return pltpu.make_async_remote_copy(
+                src_ref=src.at[at], dst_ref=held.at[at], send_sem=g_send.at[j, i],
+                recv_sem=g_recv.at[j, i], device_id=peer, device_id_type=MESH,
+            )
+
+        def own_parts(j):
+            given, held = ways[j]
+            return [
+                pltpu.make_async_copy(given.at[at], held.at[at], w_sem.at[j, i])
+                for i, at in enumerate([(my_tp, near), (my_tp, far, two), (away, near, one)])
+            ]
+
+        def late_copy(m, r):
+            src = cots[m].at[:, pl.ds(pl.multiple_of((my_z ^ r) * chunk, 16), chunk)]
             if r == 0:
-                return pltpu.make_async_copy(src, late.at[0], c_send.at[0])
+                return pltpu.make_async_copy(src, late.at[m, 0], c_send.at[m, 0])
             return pltpu.make_async_remote_copy(
-                src_ref=src, dst_ref=late.at[r], send_sem=c_send.at[r], recv_sem=c_recv.at[r],
-                device_id=to_z[r], device_id_type=MESH,
+                src_ref=src, dst_ref=late.at[m, r], send_sem=c_send.at[m, r],
+                recv_sem=c_recv.at[m, r], device_id=to_z[r], device_id_type=MESH,
             )
 
-        def cot_fetch(array, at, slot):
-            rows = pl.ds(pl.multiple_of(at * block, 8), block)
+        def cot_fetch(at, slot):
+            m, rows = at // each, pl.ds(pl.multiple_of(lax.rem(at, each) * block, 8), block)
             return pltpu.make_async_copy(
-                array.at[:, :, rows], cot_in.at[slot], cot_sem.at[slot]
+                late.at[m, :, :, rows], cot_in.at[slot], cot_sem.at[slot]
             )
 
         @pl.when(step == 0)
         def _():
+            peers = to_z[1:] + [to_core, to_x, to_y]
             barrier = pltpu.get_barrier_semaphore()
-            for peer in to_z[1:]:
+            for peer in peers:
                 pl.semaphore_signal(barrier, inc=1, device_id=peer, device_id_type=MESH)
-            pl.semaphore_wait(barrier, n_in - 1)
-            for r in range(n_in):
-                late_copy(r).start()
-            cot_fetch(cots[0], 0, 0).start()
-
-        @pl.when(jnp.logical_and(step + 1 < each, step + 1 < steps))
+            for j in range(2):
+                start_all(own_parts(j))
+            pl.semaphore_wait(barrier, len(peers))
+            for j in range(2):
+                start_all([gather(j, i) for i in range(6)])
+            start_all([late_copy(0, r) for r in range(n_in)])
+
+        for j in range(2):
+
+            @pl.when(step == count - 2 + j)
+            def _(j=j):
+                for i in range(3):
+                    gather(j, i).wait_recv()
+                start_all([gather(j, i) for i in range(6, 9)])
+
+        @pl.when(step == count - 1)
         def _():
-            cot_fetch(cots[0], step + 1, 1 - slot).start()
+            start_all([late_copy(1, r) for r in range(n_in)])
+
+        @pl.when(step == count)
+        def _():
+            for j in range(2):
+                for copy in own_parts(j):
+                    copy.wait()
+                for i in range(3, 9):
+                    gather(j, i).wait_recv()
+
+        for m in range(2):
+
+            @pl.when(step == count + m * each)
+            def _(m=m):
+                late_copy(m, 0).wait()
+                for r in range(1, n_in):
+                    late_copy(m, r).wait_recv()
+                cot_fetch(m * each, slot).start()
+
+        @pl.when(
+            jnp.logical_and(
+                step >= count,
+                jnp.logical_and(lax.rem(at_block + 1, each) != 0, at_block + 1 < count),
+            )
+        )
+        def _():
+            cot_fetch(at_block + 1, 1 - slot).start()
+
+    else:
+        at_block = 0
 
     width = out_w.shape[1]
     frames, places = results[0].shape[-3:-1]
@@ -352,122 +431,134 @@
     query_place = lax.broadcasted_iota(jnp.int32, (rows, GROUP * rows), 1) % sub
     bias = jnp.where(key_place == query_place, 0.0, -1e30)
 
-    after_space = tokens(pieces)
-    unit, rate = normalise(after_space)
-    normed_time[...] = (unit * norm[2:3] + norm[3:4]).astype(BF)
-    qkv[...] = dot(normed_time[...], qkv_w[...], NN).astype(BF)
     groups = width // WIDE
-    for j in range(parts):
-        at_rows = slice(j * rows, (j + 1) * rows)
-        for g in range(groups):
-            at = g * WIDE
-            out, logsum = attend(
-                qkv[at_rows, at : at + WIDE],
-                qkv[at_rows, width + at : width + at + WIDE],
-                qkv[at_rows, 2 * width + at : 2 * width + at + WIDE],
-                bias,
-            )
-            mixed[at_rows, at : at + WIDE] = out
-            probs_logsum[j * groups + g : j * groups + g + 1] = logsum
-    after_time = after_space + dot(mixed[...], out_w[...], NT)
-    unit2, rate2 = normalise(after_time)
-    normed_mlp[...] = (unit2 * norm[4:5] + norm[5:6]).astype(BF)
+    qkv, mixed = qkv_all.at[at_block], mixed_all.at[at_block]
+    probs_logsum, after = logsum_all.at[at_block], after_all.at[at_block]
+
+    def forward():
+        after_space = tokens(pieces)
+        unit, _ = normalise(after_space)
+        normed = (unit * norm[2:3] + norm[3:4]).astype(BF)
+        qkv[...] = dot(normed, qkv_w[...], NN).astype(BF)
+        for j in range(parts):
+            at_rows = slice(j * rows, (j + 1) * rows)
+            for g in range(groups):
+                at = g * WIDE
+                out, logsum = attend(
+                    qkv[at_rows, at : at + WIDE],
+                    qkv[at_rows, width + at : width + at + WIDE],
+                    qkv[at_rows, 2 * width + at : 2 * width + at + WIDE],
+                    bias,
+                )
+                mixed[at_rows, at : at + WIDE] = out
+                probs_logsum[j * groups + g : j * groups + g + 1] = logsum
+        after[...] = after_space + dot(mixed[...], out_w[...], NT)
+
+    def backward():
+        time_backward(after[...])
+
+    def time_backward(after_time):
+        after_space = tokens(pieces)
+        unit, rate = normalise(after_space)
+        normed_time[...] = (unit * norm[2:3] + norm[3:4]).astype(BF)
+        unit2, rate2 = normalise(after_time)
+        normed_mlp[...] = (unit2 * norm[4:5] + norm[5:6]).astype(BF)
+        if joint:
+            cot_fetch(at_block, slot).wait()
+        cot = tokens([cot_in.at[slot]] if joint else cots)
+        w_in, w_unit = (in_held, unit_held) if joint else (in_w, unit_w)
+        grad_result[...] = cot.astype(BF)
+        result = after_time
+        grad_normed = None
+        for c in range(in_w.shape[0]):
+            cols = slice(c * in_w.shape[2], (c + 1) * in_w.shape[2])
+            pre = dot(normed_mlp[...], w_in[c], NN)
+            below, density = gelu_parts(pre)
+            hidden[:, cols] = (pre * below).astype(BF)
+            result = result + dot(hidden[:, cols], w_unit[c], NT)
+            grad_hidden = dot(grad_result[...], w_unit[c], NN)
+            grad_pre[:, cols] = (grad_hidden * (below + pre * density)).astype(BF)
+            term = dot(grad_pre[:, cols], w_in[c], NT)
+            grad_normed = term if c == 0 else grad_normed + term
+        scatter(result, results)
+
+        @pl.when(at_block == 0 if joint else pl.program_id(0) == 0)
+        def _():
+            norm_out[...] = jnp.zeros_like(norm_out)
+
+        norm_out[2:3] += jnp.sum(grad_normed * unit2, axis=0, keepdims=True)
+        norm_out[3:4] += jnp.sum(grad_normed, axis=0, keepdims=True)
+        grad_after = cot + norm_back(grad_normed, norm[4:5], unit2, rate2)
+        grad_time[...] = grad_after.astype(BF)
+        grad_mixed = dot(grad_time[...], out_w[...], NN).astype(BF)
+        for j in range(parts):
+            at_rows = slice(j * rows, (j + 1) * rows)
+            for g in range(groups):
+                at = g * WIDE
+                back = attend_back(
+                    qkv[at_rows, at : at + WIDE],
+                    qkv[at_rows, width + at : width + at + WIDE],
+                    qkv[at_rows, 2 * width + at : 2 * width + at + WIDE],
+                    grad_mixed[at_rows, at : at + WIDE],
+                    probs_logsum[j * groups + g : j * groups + g + 1],
+                    bias,
+                )
+                for i, part in enumerate(back):
+                    dqkv[at_rows, i * width + at : i * width + at + WIDE] = part
+        store_columns(
+            columns,
+            [dqkv[:, i * width : (i + 1) * width] for i in range(3)] + [mixed[...]],
+            n_parts,
+        )
+        grad_normed = dot(dqkv[...], qkv_w[...], NT)
+        norm_out[0:1] += jnp.sum(grad_normed * unit, axis=0, keepdims=True)
+        norm_out[1:2] += jnp.sum(grad_normed, axis=0, keepdims=True)
+        grad_space = grad_after + norm_back(grad_normed, norm[2:3], unit, rate)
+        if not joint:
+            scatter(grad_space, grads)
+            return
+        scatter(grad_space, [outgoing.at[at_block]])
+        received = grads[0]
+        micros = received.shape[0]
+        m, at = at_block // each, pl.multiple_of(lax.rem(at_block, each) * places, 8)
+        for r in range(n_in):
+            src, dst = outgoing.at[at_block, r], received.at[m, r, :, pl.ds(at, places)]
+            if r == 0:
+                pltpu.make_async_copy(src, dst, send.at[m, 0]).start()
+            else:
+                pltpu.make_async_remote_copy(
+                    src_ref=src, dst_ref=dst, send_sem=send.at[m, r], recv_sem=recv.at[m, r],
+                    device_id=to_z[r], device_id_type=MESH,
+                ).start()
+
+        @pl.when(step == steps - 1)
+        def _():
+            for j in range(2):
+                for i in range(9):
+                    gather(j, i).wait_send()
+            for m in range(micros):
+                for r in range(1, n_in):
+                    late_copy(m, r).wait_send()
+            for m in range(micros):
+                for r in range(n_in):
+                    src = outgoing.at[pl.ds(m * each, each), r]
+                    dst = received.at[m, r]
+                    if r == 0:
+                        pltpu.make_async_copy(dst, dst, send.at[m, 0]).wait()
+                    else:
+                        for ref, wait in ((src, "wait_send"), (dst, "wait_recv")):
+                            copy = pltpu.make_async_remote_copy(
+                                src_ref=ref, dst_ref=ref, send_sem=send.at[m, r],
+                                recv_sem=recv.at[m, r], device_id=to_z[r], device_id_type=MESH,
+                            )
+                            getattr(copy, wait)()
+
     if joint:
-
-        @pl.when(step == each)
-        def _():
-            late_copy(0).wait()
-            for r in range(1, n_in):
-                late_copy(r).wait_recv()
-            cot_fetch(late, 0, slot).start()
-
-        @pl.when(jnp.logical_and(step >= each, step + 1 < steps))
-        def _():
-            cot_fetch(late, step + 1 - each, 1 - slot).start()
-
-        cot_fetch(cots[0], 0, slot).wait()
-    cot = tokens([cot_in.at[slot]] if joint else cots)
-    grad_result[...] = cot.astype(BF)
-    result = after_time
-    grad_normed = None
-    for c in range(in_w.shape[0]):
-        cols = slice(c * in_w.shape[2], (c + 1) * in_w.shape[2])
-        pre = dot(normed_mlp[...], in_w[c], NN)
-        below, density = gelu_parts(pre)
-        hidden[:, cols] = (pre * below).astype(BF)
-        result = result + dot(hidden[:, cols], unit_w[c], NT)
-        grad_hidden = dot(grad_result[...], unit_w[c], NN)
-        grad_pre[:, cols] = (grad_hidden * (below + pre * density)).astype(BF)
-        term = dot(grad_pre[:, cols], in_w[c], NT)
-        grad_normed = term if c == 0 else grad_normed + term
-    scatter(result, results)
-
-    @pl.when(pl.program_id(0) == 0)
-    def _():
-        norm_out[...] = jnp.zeros_like(norm_out)
-
-    norm_out[2:3] += jnp.sum(grad_normed * unit2, axis=0, keepdims=True)
-    norm_out[3:4] += jnp.sum(grad_normed, axis=0, keepdims=True)
-    grad_after = cot + norm_back(grad_normed, norm[4:5], unit2, rate2)
-    grad_time[...] = grad_after.astype(BF)
-    grad_mixed = dot(grad_time[...], out_w[...], NN).astype(BF)
-    for j in range(parts):
-        at_rows = slice(j * rows, (j + 1) * rows)
-        for g in range(groups):
-            at = g * WIDE
-            back = attend_back(
-                qkv[at_rows, at : at + WIDE],
-                qkv[at_rows, width + at : width + at + WIDE],
-                qkv[at_rows, 2 * width + at : 2 * width + at + WIDE],
-                grad_mixed[at_rows, at : at + WIDE],
-                probs_logsum[j * groups + g : j * groups + g + 1],
-                bias,
-            )
-            for i, part in enumerate(back):
-                dqkv[at_rows, i * width + at : i * width + at + WIDE] = part
-    store_columns(
-        columns,
-        [dqkv[:, i * width : (i + 1) * width] for i in range(3)] + [mixed[...]],
-        n_parts,
-    )
-    grad_normed = dot(dqkv[...], qkv_w[...], NT)
-    norm_out[0:1] += jnp.sum(grad_normed * unit, axis=0, keepdims=True)
-    norm_out[1:2] += jnp.sum(grad_normed, axis=0, keepdims=True)
-    grad_space = grad_after + norm_back(grad_normed, norm[2:3], unit, rate)
-    if not joint:
-        scatter(grad_space, grads)
-        return
-    scatter(grad_space, [outgoing.at[step]])
-    received = grads[0]
-    micros = received.shape[0]
-    m, at = step // each, pl.multiple_of(lax.rem(step, each) * places, 8)
-    for r in range(n_in):
-        src, dst = outgoing.at[step, r], received.at[m, r, :, pl.ds(at, places)]
-        if r == 0:
-            pltpu.make_async_copy(src, dst, send.at[m, 0]).start()
-        else:
-            pltpu.make_async_remote_copy(
-                src_ref=src, dst_ref=dst, send_sem=send.at[m, r], recv_sem=recv.at[m, r],
-                device_id=to_z[r], device_id_type=MESH,
-            ).start()
-
-    @pl.when(step == steps - 1)
-    def _():
-        for r in range(1, n_in):
-            late_copy(r).wait_send()
-        for m in range(micros):
-            for r in range(n_in):
-                src = outgoing.at[pl.ds(m * each, each), r]
-                dst = received.at[m, r]
-                if r == 0:
-                    pltpu.make_async_copy(dst, dst, send.at[m, 0]).wait()
-                else:
-                    for ref, wait in ((src, "wait_send"), (dst, "wait_recv")):
-                        copy = pltpu.make_async_remote_copy(
-                            src_ref=ref, dst_ref=ref, send_sem=send.at[m, r],
-                            recv_sem=recv.at[m, r], device_id=to_z[r], device_id_type=MESH,
-                        )
-                        getattr(copy, wait)()
+        pl.when(step < count)(forward)
+        pl.when(step >= count)(backward)
+    else:
+        forward()
+        backward()
 
 
 def time_layer(pieces, cots, qkv_w, out_w, in_w, unit_w, norm):
@@ -483,43 +574,59 @@
     hidden = in_w.shape[0] * in_w.shape[2]
     whole = pl.BlockSpec(memory_space=pltpu.VMEM)
     if joint:
-        piece = pl.BlockSpec(
-            (None, n_in, frames, block, width), lambda b: (b // each, 0, 0, b % each, 0)
-        )
+        blocks_all = micros * each
+
+        def joint_piece(place):
+            return pl.BlockSpec(
+                (None, n_in, frames, block, width),
+                lambda b: (place(b) // each, 0, 0, place(b) % each, 0),
+            )
+
+        piece = joint_piece(lambda b: b % blocks_all)
         any_spec = pl.BlockSpec(memory_space=pl.ANY)
-        given = [piece, any_spec, any_spec]
-        moved = [piece, any_spec, any_spec]
+        later = lambda b: jnp.maximum(b - blocks_all, 0)
+        given = [piece, any_spec, any_spec, whole, whole, any_spec, any_spec, whole]
+        moved = [joint_piece(later), any_spec, any_spec]
+        row = lambda cols: pl.BlockSpec((tokens, cols), lambda b: (later(b), 0))
     else:
         piece = pl.BlockSpec((frames, block, width), lambda b: (0, b, 0))
-        given = moved = [piece] * (2 * n_in)
-    row = lambda cols: pl.BlockSpec((tokens, cols), lambda b: (b, 0))
+        moved = [piece] * (2 * n_in)
+        given = moved + [whole] * 5
+        row = lambda cols: pl.BlockSpec((tokens, cols), lambda b: (b, 0))
     kept = [width, 4 * width, width, width, hidden, hidden, width]
     dma = pltpu.SemaphoreType.DMA
+    n_kept = micros * each if joint else 1
     sending = [
         pltpu.VMEM((micros * each, n_in, frames, block, width), BF),
         pltpu.VMEM((2, n_in, frames, block, width), BF),
+        pltpu.VMEM(in_w.shape, BF),
+        pltpu.VMEM(unit_w.shape, BF),
         dma((micros, n_in)),
         dma((micros, n_in)),
-        dma((n_in,)),
-        dma((n_in,)),
+        dma((micros, n_in)),
+        dma((micros, n_in)),
         dma((2,)),
+        dma((2, 9)),
+        dma((2, 9)),
+        dma((2, 3)),
     ]
     sent = [jax.ShapeDtypeStruct(a.shape, BF) for a in pieces + cots]
     if joint:
-        sent = [jax.ShapeDtypeStruct(a.shape, BF) for a in (pieces[0], pieces[0], cots[0])]
+        sent = [jax.ShapeDtypeStruct(pieces[0].shape, BF)] * 3
     return pl.pallas_call(
         partial(time_kernel, joint, n_in, in_w.shape[0], sub),
-        grid=(micros * each,),
-        in_specs=given + [whole] * 5,
+        grid=(2 * micros * each if joint else each,),
+        in_specs=given,
         out_specs=moved + [row(cols) for cols in kept] + [pl.BlockSpec((4, width), lambda b: (0, 0))],
         out_shape=sent
         + [jax.ShapeDtypeStruct((count, cols), BF) for cols in kept]
         + [jax.ShapeDtypeStruct((4, width), F32)],
         scratch_shapes=[
+            pltpu.VMEM((n_kept, tokens, 3 * width), BF),
             pltpu.VMEM((tokens, 3 * width), BF),
-            pltpu.VMEM((tokens, 3 * width), BF),
-            pltpu.VMEM((tokens, width), BF),
-            pltpu.VMEM((8 * (block // sub), GROUP * frames * n_in * sub), F32),
+            pltpu.VMEM((n_kept, tokens, width), BF),
+            pltpu.VMEM((n_kept, 8 * (block // sub), GROUP * frames * n_in * sub), F32),
+            pltpu.VMEM((n_kept, tokens, width), F32),
         ]
         + (sending if joint else []),
         compiler_params=pltpu.CompilerParams(
@@ -1088,9 +1195,9 @@
 
 def front_kernel(
     inputs, cot, shard, ln_shard,
-    xs_out, time_in, cots, cot_late, qkv_out, mixed_out, logsum_out,
+    xs_out, time_in, cot_half, cot_late, qkv_out, mixed_out, logsum_out,
     qkv_a, out_a, qkv_b, out_b, in_w, unit_w, norms,
-    xs, sent, raw, std_qkv, std_out, ln, cot_half, qkv, mixed,
+    xs, sent, raw, std_qkv, std_out, ln, qkv, mixed,
     send, recv, t_send, t_recv, local,
 ):
     my_tp, my_y, my_z = lax.axis_index("tp"), lax.axis_index("clip"), lax.axis_index("fp")
@@ -1124,7 +1231,7 @@
     near = pl.multiple_of(my_y * half, 16)
     far = pl.multiple_of((1 - my_y) * half, 16)
     away = my_tp ^ 2
-    cuts = [cols // 2] + [5 * cols // 6] * 3
+    cuts = [cols // 2, 5 * cols // 6, cols // 2, cols // 2]
     own_shards = []
     by_z, by_x, by_y, by_y2, by_x2, by_core = [], [], [], [], [], []
     for j, tile in enumerate(tiles):
@@ -1142,22 +1249,21 @@
             ]
         )
         by_x.append(same(to_x, my_tp, near_rows, one))
+        by_y2.append(same(to_y, my_tp, near_rows, two))
+        if j >= 2:
+            continue
         by_y.append([same(to_y, my_tp, near_rows, one), same(to_y, away, near_rows, one)])
+        by_x2.append(same(to_x, my_tp, slice(None), two))
         by_core.append(
             [
                 same(to_core, my_tp, near_rows),
                 same(to_core, away, near_rows, one),
                 same(to_core, my_tp, far_rows, one),
                 same(to_core, away, far_rows, one),
-            ]
-        )
-        if cut < cols:
-            by_y2.append(same(to_y, my_tp, near_rows, two))
-            by_x2.append(same(to_x, my_tp, slice(None), two))
-            by_core[j] += [
                 same(to_core, my_tp, far_rows, two),
                 same(to_core, away, slice(None), two),
             ]
+        )
     ln_z = [
         remote.add(ln_shard, ln.at[pl.ds(mine, own)], to_z[r]) for r in range(1, n_z)
     ]
@@ -1180,15 +1286,6 @@
         ]
         for m, half in enumerate((cot_half, cot_late))
     ]
-    cot_z = [
-        remote.add(
-            cot_half.at[:, pl.ds(pl.multiple_of((my_z ^ r) * chunk, 16), chunk)],
-            cots.at[r],
-            to_z[r],
-        )
-        for r in range(1, n_z)
-    ]
-
     own_x = [
         here(inputs.at[m, my_tp], xs.at[pl.ds(m * frames, frames), pl.ds(0, part)])
         for m in range(micros)
@@ -1208,7 +1305,8 @@
         arrive(by_z[j])
         by_x[j].start()
         by_y2[j].start()
-        by_core[j][0].start()
+        if j < 2:
+            by_core[j][0].start()
 
     def gather_first(j):
         by_x[j].wait_recv()
@@ -1258,23 +1356,10 @@
     weights_out = [here(std_qkv.at[0], qkv_a), here(std_out.at[0], out_a)]
 
     def frame(f, carry):
-        @pl.when(f == 2)
-        def _():
-            own_cot[0].wait()
-            arrive(cot_in[0])
-            start_all(cot_z)
-            gather_second(2)
-            gather_second(3)
-
         @pl.when(f == frames)
         def _():
             own_x[1].wait()
             arrive(x_in[1])
-            gather_first(2)
-
-        @pl.when(f == frames + 2)
-        def _():
-            gather_first(3)
             start_all(cot_in[1])
 
         x = xs[f].astype(F32)
@@ -1311,16 +1396,12 @@
     arrive(by_core[1])
     standard(1)
     weights_out += [here(std_qkv.at[1], qkv_b), here(std_out.at[1], out_b)]
-    own_cots = [
-        here(cot_half.at[:, pl.ds(pl.multiple_of(my_z * chunk, 16), chunk)], cots.at[0])
-    ]
-    gather_last(2)
-    gather_last(3)
-    arrive(by_core[2])
-    arrive(by_core[3])
-    own_cot[1].wait()
-    arrive(cot_in[1])
-    arrive(cot_z)
+    for j in (2, 3):
+        by_x[j].wait_recv()
+        by_y2[j].wait_recv()
+    for m in range(micros):
+        own_cot[m].wait()
+        arrive(cot_in[m])
     for m in range(micros):
         for r in range(n_z):
             src = sent.at[
@@ -1336,7 +1417,7 @@
                 ).wait()
     for copy in remote.all:
         copy.wait_send()
-    for copy in kept + weights_out + own_cots:
+    for copy in kept + weights_out:
         copy.wait()
 
 
@@ -1360,7 +1441,7 @@
         out_shape=[
             shape((total, places, width), BF),
             shape((micros, n_z, frames, chunk, width), BF),
-            shape((n_z, frames, chunk, width), BF),
+            shape((frames, places, width), BF),
             shape((frames, places, width), BF),
             shape((total, places, 3 * width), BF),
             shape((total, places, width), BF),
@@ -1375,7 +1456,6 @@
             pltpu.VMEM((2, width, 3 * width), BF),
             pltpu.VMEM((2, width, width), BF),
             pltpu.VMEM((width, ln_shard.shape[1]), BF),
-            pltpu.VMEM((frames, places, width), BF),
             pltpu.VMEM((total, places, 3 * width), BF),
             pltpu.VMEM((total, places, width), BF),
             dma((N_REMOTE,)),
@@ -1461,11 +1541,11 @@
         ln_shard = jnp.stack(ln_rows + [jnp.zeros_like(ln_rows[0])] * 122, axis=1)
         shard = jnp.stack([first, second, mlp_in, mlp_out.T])
         (
-            xs, time_pieces, cots, cot_late, qkv, mixed, logsum,
+            xs, time_pieces, cot_half, cot_late, qkv, mixed, logsum,
             qkv_space_w, out_space_w, qkv_time_w, out_time_w, in_w, unit_w, norms,
         ) = front(inputs, cotangent, shard, ln_shard)
         results, grads, _, *kept, tail = time_layer(
-            [time_pieces], [cots, cot_late], qkv_time_w, out_time_w, in_w, unit_w, norms
+            [time_pieces], [cot_half, cot_late], qkv_time_w, out_time_w, in_w, unit_w, norms
         )
         sums, norm_grads, acts, input_grad, *_ = back(
             results, grads, xs, qkv, mixed, logsum, qkv_space_w, out_space_w, norms, tail, kept

time: 451 us -> 434 us (0.962)
  Pallas kernels: 428 us -> 412 us
    pallas_call x1, Pallas kernels: 140 us -> 115 us  [front(): pl.pallas_call(front_kernel, in_specs=[any_spec] * 4, out_specs=[any_spec...]
    pallas_call x1, Pallas kernels: 117 us -> 126 us  [time_layer(): pl.pallas_call(partial(time_kernel, joint, n_in, in_w.shape[0], sub), gri...]
where the time goes in v1:
time: 434 us; the launch traced here: 429 us
  Pallas kernels  412 us (95%)
  local copies, waits for them, and re-layouts  10.9 us (3%)
  other arithmetic  5.68 us (1%)
    pallas_call x1, Pallas kernels, back(): pl.pallas_call(back_kernel, in_specs=[any_spec] * 9 + [vmem] + [any_spec]...  170 us
    pallas_call x1, Pallas kernels, time_layer(): pl.pallas_call(partial(time_kernel, joint, n_in, in_w.shape[0], sub), gri...  126 us
    pallas_call x1, Pallas kernels, front(): pl.pallas_call(front_kernel, in_specs=[any_spec] * 4, out_specs=[any_spec...  115 us

profile of v1, /device:TPU:0, one launch (start us, length us, event | category | flops | bytes accessed | tf_op | source)
XLA Modules:
  0.0 429.4 jit_solution(8691598832832279986)
XLA Ops:
  0.6 0.0 copy-start.3
  0.7 0.0 copy-start.4
  0.7 0.9 slice_bitcast_fusion.17
  1.6 0.9 copy.18
  2.5 0.9 copy.19
  3.4 0.1 maximum_bitcast_fusion.2
  3.5 1.9 pad_maximum_fusion.shard
  5.4 0.0 copy-done.3
  5.4 0.1 copy.20
  5.6 0.0 copy-done.4
  5.6 0.1 copy.21
  5.7 0.1 copy.22
  5.8 0.1 copy.23
  5.9 0.1 copy.24
  6.1 0.1 copy.25
  6.3 0.8 stack.76.ln_shard
  7.0 115.4 %shard_map.160 = (bf16[8,192,768]{2,1,0:T(8,128)(2,1)}, bf16[2,4,4,48,768]{4,3,2,1,0:T(8,128)(2,1)}, bf16[4,192,768]{2,1,0:T(8,128)(2,1)}, bf16[4,192,768]{2,1,0...) custom-call(bf16[2,4,4,48,768]{4,3,2,1,0:T(8,128)(2,1)} %inputs.1, ...), custom_call_target="tpu_custom_call" | custom-call | flops 9059696640 | bytes 18874368 | tf_op jit(solution)/shard_map/pallas_call | solution.py:1437
  122.4 126.4 %shard_map.161 = (bf16[2,4,4,48,768]{4,3,2,1,0:T(8,128)(2,1)}, bf16[2,4,4,48,768]{4,3,2,1,0:T(8,128)(2,1)}, bf16[2,4,4,48,768]{4,3,2,1,0:T(8,128)(2,1)}, bf16[15...) custom-call(bf16[2,4,4,48,768]{4,3,2,1,0:T(8,128)(2,1)} %get-tuple-e, ...), custom_call_target="tpu_custom_call" | custom-call | flops 43486543872 | bytes 39936000 | tf_op jit(solution)/shard_map/pallas_call | solution.py:616
  248.8 169.9 %shard_map.162 = (f32[4,96,768]{2,1,0:T(8,128)}, f32[8,768]{1,0:T(8,128)}, bf16[2,4,4,48,768]{4,3,2,1,0:T(8,128)(2,1)}, bf16[2,4,4,48,768]{4,3,2,1,0:T(8,128)(2,...) custom-call(bf16[2,4,4,48,768]{4,3,2,1,0:T(8,128)(2,1)} %get-tuple-e, ...), custom_call_target="tpu_custom_call" | custom-call | flops 41674604544 | bytes 70778880 | tf_op jit(solution)/shard_map/pallas_call | solution.py:1134
  418.8 2.1 slice_bitcast_fusion
  420.9 0.0 copy-start
  420.9 0.1 slice_bitcast_fusion.5
  421.0 0.1 slice_bitcast_fusion.4
  421.2 0.9 pad_maximum_fusion.1
  422.1 0.7 copy-done
  422.8 0.0 copy-start.2
  422.8 0.0 copy-start.1
  422.8 2.8 convert_element_type.3
  425.6 0.7 copy.27
  426.3 0.7 copy.28
  427.0 0.0 copy-done.2
  427.0 0.1 reshape.21
  427.1 0.6 slice_bitcast_fusion.18
  427.7 0.0 copy-done.1
  427.7 1.4 copy.32
  (11 shorter events, 0.1 us)
Async XLA Ops:
  0.6 4.8 %copy-start.3 = (bf16[3,96]{1,0:T(4,128)(2,1)S(1)}, bf16[3,96]{1,0:T(4,128)(2,1)}, u32[]{:S(2)}) copy-start(bf16[3,96]{1,0:T(4,128)(2,1)} %param.16) | copy-start | bytes 1732
  0.7 4.9 %copy-start.4 = (bf16[3,96]{1,0:T(4,128)(2,1)S(1)}, bf16[3,96]{1,0:T(4,128)(2,1)}, u32[]{:S(2)}) copy-start(bf16[3,96]{1,0:T(4,128)(2,1)} %param.17) | copy-start | bytes 1732
  420.9 1.9 copy-start
  422.8 4.3 copy-start.2
  422.8 4.9 %copy-start.1 = (bf16[2,4,4,48,768]{4,3,2,1,0:T(8,128)(2,1)S(1)}, bf16[2,4,4,48,768]{4,3,2,1,0:T(8,128)(2,1)}, u32[]{:S(2)}) copy-start(bf16[2,4,4,48,768]{4,3,2,1,0:T(8,128)(2,1)} %get-tuple-element.111) | copy-start | bytes 7077892

commit v2 on v1

--- a/solution.py
+++ b/solution.py
@@ -354,13 +354,16 @@
             for j in range(2):
                 start_all(own_parts(j))
             pl.semaphore_wait(barrier, len(peers))
-            for j in range(2):
-                start_all([gather(j, i) for i in range(6)])
+            start_all([gather(0, i) for i in range(6)])
             start_all([late_copy(0, r) for r in range(n_in)])
 
+        @pl.when(step == 1)
+        def _():
+            start_all([gather(1, i) for i in range(6)])
+
         for j in range(2):
 
-            @pl.when(step == count - 2 + j)
+            @pl.when(step == count - 3 + 2 * j)
             def _(j=j):
                 for i in range(3):
                     gather(j, i).wait_recv()
@@ -983,10 +986,6 @@
         def _():
             after_second(0)
 
-        @pl.when(f == 6)
-        def _():
-            after_second(1)
-
         @pl.when(f == 7)
         def _():
             after_third(0)
@@ -1065,8 +1064,7 @@
     turn(3, todo)
     product(0, last)
     product(1, last)
-    after_second(2)
-    after_third(1)
+    after_second(1)
     tails[0].wait_recv()
     tail_sum[1] = tail_sum[0] + tail_got[0]
     tails[1].start()
@@ -1079,15 +1077,17 @@
     tails[1].wait_recv()
     tail_sum[2] = tail_sum[1] + tail_got[1]
     tails[2].start()
-    after_third(2)
+    after_second(2)
     after_second(3)
     after_second(4)
+    after_third(1)
     after_fourth(1)
     tails[2].wait_recv()
     tail_sum[3] = tail_sum[2] + tail_got[2]
     start_all(tails[3:])
     after_third(3)
     after_third(4)
+    after_third(2)
     after_fourth(2)
     value = tail_sum[3]
     for r in range(n_z - 1):

time: 434 us -> 446 us (1.028)
  Pallas kernels: 412 us -> 423 us
    pallas_call x1, Pallas kernels: 170 us -> 182 us  [back(): pl.pallas_call(back_kernel, in_specs=[any_spec] * 9 + [vmem] + [any_spec]...]
where the time goes in v2:
time: 446 us; the launch traced here: 441 us
  Pallas kernels  423 us (95%)
  local copies, waits for them, and re-layouts  10.9 us (2%)
  other arithmetic  5.68 us (1%)
    pallas_call x1, Pallas kernels, back(): pl.pallas_call(back_kernel, in_specs=[any_spec] * 9 + [vmem] + [any_spec]...  182 us
    pallas_call x1, Pallas kernels, time_layer(): pl.pallas_call(partial(time_kernel, joint, n_in, in_w.shape[0], sub), gri...  126 us
    pallas_call x1, Pallas kernels, front(): pl.pallas_call(front_kernel, in_specs=[any_spec] * 4, out_specs=[any_spec...  115 us

profile of v2, /device:TPU:0, one launch (start us, length us, event | category | flops | bytes accessed | tf_op | source)
XLA Modules:
  0.0 441.1 jit_solution(7498434274809790630)
XLA Ops:
  0.6 0.0 copy-start.3
  0.7 0.0 copy-start.4
  0.7 0.9 slice_bitcast_fusion.17
  1.6 0.9 copy.18
  2.5 0.9 copy.19
  3.4 0.1 maximum_bitcast_fusion.2
  3.5 1.9 pad_maximum_fusion.shard
  5.4 0.0 copy-done.3
  5.4 0.1 copy.20
  5.6 0.0 copy-done.4
  5.6 0.1 copy.21
  5.7 0.1 copy.22
  5.8 0.1 copy.23
  5.9 0.1 copy.24
  6.1 0.1 copy.25
  6.3 0.8 stack.76.ln_shard
  7.0 115.4 %shard_map.160 = (bf16[8,192,768]{2,1,0:T(8,128)(2,1)}, bf16[2,4,4,48,768]{4,3,2,1,0:T(8,128)(2,1)}, bf16[4,192,768]{2,1,0:T(8,128)(2,1)}, bf16[4,192,768]{2,1,0...) custom-call(bf16[2,4,4,48,768]{4,3,2,1,0:T(8,128)(2,1)} %inputs.1, ...), custom_call_target="tpu_custom_call" | custom-call | flops 9059696640 | bytes 18874368 | tf_op jit(solution)/shard_map/pallas_call | solution.py:1437
  122.4 126.5 %shard_map.161 = (bf16[2,4,4,48,768]{4,3,2,1,0:T(8,128)(2,1)}, bf16[2,4,4,48,768]{4,3,2,1,0:T(8,128)(2,1)}, bf16[2,4,4,48,768]{4,3,2,1,0:T(8,128)(2,1)}, bf16[15...) custom-call(bf16[2,4,4,48,768]{4,3,2,1,0:T(8,128)(2,1)} %get-tuple-e, ...), custom_call_target="tpu_custom_call" | custom-call | flops 43486543872 | bytes 39936000 | tf_op jit(solution)/shard_map/pallas_call | solution.py:619
  248.9 181.6 %shard_map.162 = (f32[4,96,768]{2,1,0:T(8,128)}, f32[8,768]{1,0:T(8,128)}, bf16[2,4,4,48,768]{4,3,2,1,0:T(8,128)(2,1)}, bf16[2,4,4,48,768]{4,3,2,1,0:T(8,128)(2,...) custom-call(bf16[2,4,4,48,768]{4,3,2,1,0:T(8,128)(2,1)} %get-tuple-e, ...), custom_call_target="tpu_custom_call" | custom-call | flops 41674604544 | bytes 70778880 | tf_op jit(solution)/shard_map/pallas_call | solution.py:1134
  430.5 2.1 slice_bitcast_fusion
  432.6 0.0 copy-start
  432.6 0.1 slice_bitcast_fusion.5
  432.8 0.1 slice_bitcast_fusion.4
  432.9 0.9 pad_maximum_fusion.1
  433.8 0.7 copy-done
  434.5 0.0 copy-start.2
  434.5 0.0 copy-start.1
  434.5 2.8 convert_element_type.3
  437.3 0.7 copy.27
  438.0 0.7 copy.28
  438.8 0.0 copy-done.2
  438.8 0.1 reshape.21
  438.9 0.6 slice_bitcast_fusion.18
  439.5 0.0 copy-done.1
  439.5 1.4 copy.32
  (11 shorter events, 0.1 us)
Async XLA Ops:
  0.6 4.8 %copy-start.3 = (bf16[3,96]{1,0:T(4,128)(2,1)S(1)}, bf16[3,96]{1,0:T(4,128)(2,1)}, u32[]{:S(2)}) copy-start(bf16[3,96]{1,0:T(4,128)(2,1)} %param.16) | copy-start | bytes 1732
  0.7 4.9 %copy-start.4 = (bf16[3,96]{1,0:T(4,128)(2,1)S(1)}, bf16[3,96]{1,0:T(4,128)(2,1)}, u32[]{:S(2)}) copy-start(bf16[3,96]{1,0:T(4,128)(2,1)} %param.17) | copy-start | bytes 1732
  432.6 1.9 copy-start
  434.5 4.3 copy-start.2
  434.5 4.9 %copy-start.1 = (bf16[2,4,4,48,768]{4,3,2,1,0:T(8,128)(2,1)S(1)}, bf16[2,4,4,48,768]{4,3,2,1,0:T(8,128)(2,1)}, u32[]{:S(2)}) copy-start(bf16[2,4,4,48,768]{4,3,2,1,0:T(8,128)(2,1)} %get-tuple-element.111) | copy-start | bytes 7077892
